TPU v7x, 128 devices: a whole 4x4x4 slice. The times are simulated.
128 devices in a mesh: frame: 32 (over z_lo, x, y), fsdp: 4 (over z_hi, core).
Axes of the slice: x: 4, y: 4, z: 4 (z_hi: 2, z_lo: 2; z = z_hi * 2 + z_lo), core: 2. Of those that a mesh axis runs over, the one named last changes fastest.
Arguments:
- frames_in: bfloat16 [8, 32, 256, 1024], P('fsdp', 'frame'), may hold values from -6 to 6
- sp_qkv: bfloat16 [1024, 3072], P('fsdp'), may hold values from -1 to 1
- sp_out: bfloat16 [1024, 1024], P('fsdp'), may hold values from -0.1875 to 0.1875
- tm_qkv: bfloat16 [1024, 3072], P('fsdp'), may hold values from -1 to 1
- tm_out: bfloat16 [1024, 1024], P('fsdp'), may hold values from -0.1875 to 0.1875
- cotangent: bfloat16 [8, 32, 256, 1024], P('fsdp', None, 'frame'), may hold values from -6 to 6
Outputs:
- block_out: bfloat16 [8, 32, 256, 1024], P('fsdp', None, 'frame')
- grad_in: float32 [8, 32, 256, 1024], P('fsdp', 'frame')
- grad_tm_qkv: float32 [1024, 3072], P('fsdp')
All inputs are finite; a program needn't handle non-finite values.
Results may differ from a plain program's by a relative error of at most 0.035.
Values may be sent and summed in bfloat16 or wider, within the bound.
A program may use at most 192 MiB of HBM per device.

v0:
```python
import jax
import jax.numpy as jnp
from jax import lax
from jax.sharding import PartitionSpec as P

HEADS = 8


EPS = 1e-05


def normalize(u):
    mean = jnp.mean(u, axis=-1, keepdims=True)
    cent = u - mean
    rstd = lax.rsqrt(jnp.mean(cent * cent, axis=-1, keepdims=True) + EPS)
    return (cent * rstd, rstd)


def norm_back(normed, rstd, grad):
    first = jnp.mean(grad, axis=-1, keepdims=True)
    second = jnp.mean(grad * normed, axis=-1, keepdims=True)
    return rstd * (grad - first - normed * second)


def times(left, weight):
    flat = left.reshape(-1, left.shape[-1])
    prod = jnp.dot(flat, weight, preferred_element_type=jnp.float32)
    return prod.reshape(left.shape[:-1] + (weight.shape[1],))


def times_t(left, weight):
    flat = left.reshape(-1, left.shape[-1])
    prod = lax.dot_general(
        flat, weight, (((1,), (1,)), ((), ())), preferred_element_type=jnp.float32
    )
    return prod.reshape(left.shape[:-1] + (weight.shape[0],))


def split_heads(packed, heads):
    width = packed.shape[-1] // 3
    shape = packed.shape[:-1] + (heads, width // heads)
    return [packed[..., i * width : (i + 1) * width].reshape(shape) for i in range(3)]


def attend(query, keys, values, causal):
    scale = query.shape[-1] ** (-0.5)
    scores = (
        jnp.einsum("blxhe,bmxhe->bxhlm", query, keys, preferred_element_type=jnp.float32) * scale
    )
    if causal:
        steps = scores.shape[-1]
        allowed = jnp.arange(steps)[:, None] >= jnp.arange(steps)[None, :]
        scores = jnp.where(allowed, scores, -jnp.inf)
    top = jnp.max(scores, axis=-1, keepdims=True)
    expo = jnp.exp(scores - top)
    probs = expo / jnp.sum(expo, axis=-1, keepdims=True)
    lowered = probs.astype(jnp.bfloat16)
    att = jnp.einsum("bxhlm,bmxhe->blxhe", lowered, values, preferred_element_type=jnp.float32)
    return (att.astype(jnp.bfloat16), probs, lowered)


def attend_back(query, keys, values, probs, lowered, grad_att):
    scale = query.shape[-1] ** (-0.5)
    d_probs = jnp.einsum("blxhe,bmxhe->bxhlm", grad_att, values, preferred_element_type=jnp.float32)
    d_values = jnp.einsum(
        "bxhlm,blxhe->bmxhe", lowered, grad_att, preferred_element_type=jnp.float32
    )
    d_scores = probs * (d_probs - jnp.sum(d_probs * probs, axis=-1, keepdims=True)) * scale
    d_low = d_scores.astype(jnp.bfloat16)
    d_query = jnp.einsum("bxhlm,bmxhe->blxhe", d_low, keys, preferred_element_type=jnp.float32)
    d_keys = jnp.einsum("bxhlm,blxhe->bmxhe", d_low, query, preferred_element_type=jnp.float32)
    return (d_query, d_keys, d_values)


def join_heads(parts, shape):
    return jnp.concatenate([p.reshape(shape) for p in parts], axis=-1).astype(jnp.bfloat16)


def body(frames_in, sp_qkv, sp_out, tm_qkv, tm_out, cotangent):
    clips, frames_local, tokens_frame, width = frames_in.shape
    sp_qkv_all, sp_out_all = (
        lax.all_gather(sp_qkv, "fsdp", axis=0, tiled=True),
        lax.all_gather(sp_out, "fsdp", axis=0, tiled=True),
    )
    tm_qkv_all, tm_out_all = (
        lax.all_gather(tm_qkv, "fsdp", axis=0, tiled=True),
        lax.all_gather(tm_out, "fsdp", axis=0, tiled=True),
    )
    normed_one, rstd_one = normalize(frames_in.astype(jnp.float32))
    spatial_qkv = times(normed_one.astype(jnp.bfloat16), sp_qkv_all).astype(jnp.bfloat16)
    sq, sk, sv = split_heads(
        spatial_qkv.reshape(clips * frames_local, tokens_frame, 1, 3 * width), HEADS
    )
    spatial_att, sp_probs, sp_low = attend(sq, sk, sv, False)
    spatial_att = spatial_att.reshape(frames_in.shape)
    stream = (frames_in.astype(jnp.float32) + times(spatial_att, sp_out_all)).astype(jnp.bfloat16)
    stream = lax.optimization_barrier(stream)
    normed_two, rstd_two = normalize(stream.astype(jnp.float32))
    low_two = normed_two.astype(jnp.bfloat16)
    temporal_qkv = times(low_two, tm_qkv_all).astype(jnp.bfloat16)
    stream_pos, qkv_pos = (
        lax.all_to_all(stream, "frame", split_axis=2, concat_axis=1, tiled=True),
        lax.all_to_all(temporal_qkv, "frame", split_axis=2, concat_axis=1, tiled=True),
    )
    tq, tk, tv = split_heads(qkv_pos, HEADS)
    temporal_att, tm_probs, tm_low = attend(tq, tk, tv, True)
    temporal_att = temporal_att.reshape(stream_pos.shape)
    block_out = (stream_pos.astype(jnp.float32) + times(temporal_att, tm_out_all)).astype(
        jnp.bfloat16
    )
    d_temporal_att = times_t(cotangent, tm_out_all).astype(jnp.bfloat16)
    parts = attend_back(tq, tk, tv, tm_probs, tm_low, d_temporal_att.reshape(tq.shape))
    d_qkv_pos = join_heads(parts, stream_pos.shape)
    d_qkv_frame, cot_frame = (
        lax.all_to_all(d_qkv_pos, "frame", split_axis=1, concat_axis=2, tiled=True),
        lax.all_to_all(cotangent, "frame", split_axis=1, concat_axis=2, tiled=True),
    )
    d_stream = cot_frame.astype(jnp.float32) + norm_back(
        normed_two, rstd_two, times_t(d_qkv_frame, tm_qkv_all)
    )
    left_rows = low_two.reshape(-1, width)
    right_rows = d_qkv_frame.reshape(-1, 3 * width)
    shard = lax.psum_scatter(
        lax.dot_general(
            left_rows, right_rows, (((0,), (0,)), ((), ())), preferred_element_type=jnp.float32
        ).astype(jnp.bfloat16),
        "fsdp",
        scatter_dimension=0,
        tiled=True,
    )
    grad_tm_qkv = lax.psum(shard, "frame").astype(jnp.float32)
    d_spatial_att = times_t(d_stream.astype(jnp.bfloat16), sp_out_all).astype(jnp.bfloat16)
    parts = attend_back(sq, sk, sv, sp_probs, sp_low, d_spatial_att.reshape(sq.shape))
    d_spatial_qkv = join_heads(parts, frames_in.shape)
    grad_in = d_stream + norm_back(normed_one, rstd_one, times_t(d_spatial_qkv, sp_qkv_all))
    return (block_out, grad_in, grad_tm_qkv)


def solution(mesh):
    in_specs = (
        P("fsdp", "frame", None, None),
        P("fsdp", None),
        P("fsdp", None),
        P("fsdp", None),
        P("fsdp", None),
        P("fsdp", None, "frame", None),
    )
    out_specs = (P("fsdp", None, "frame", None), P("fsdp", "frame", None, None), P("fsdp", None))
    return jax.shard_map(body, mesh=mesh, in_specs=in_specs, out_specs=out_specs, check_vma=False)
```

profile of v0, /device:TPU:0, one launch (start us, length us, event | category | flops | bytes accessed | tf_op | source)
XLA Modules:
  0.0 719.7 jit_solution(1000257270924355473)
XLA Ops:
  10.6 52.1 %all-gather.5.cloned.1.call-done = bf16[1024,3072]{1,0:T(8,128)(2,1)} async-done(((bf16[256,3072]{1,0:T(8,128)(2,1)}), bf16[1024,3072]{1,0:T(8,128)(2,1)}) %all-gather.5.cloned.1.call-update) | async-done | bytes 6291472 | tf_op jit(solution)/shard_map/all_gather | solution.py:82
  62.8 6.6 fusion.18
  74.9 5.1 fusion.181
  82.8 7.6 %all-gather.7.cloned.1.call-done = bf16[1024,1024]{1,0:T(8,128)(2,1)} async-done(((bf16[256,1024]{1,0:T(8,128)(2,1)}), bf16[1024,1024]{1,0:T(8,128)(2,1)}) %all-gather.7.cloned.1.call-update) | async-done | bytes 2097168 | tf_op jit(solution)/shard_map/all_gather | solution.py:83
  94.3 47.6 %all-gather.9.cloned.1.call-done = bf16[1024,3072]{1,0:T(8,128)(2,1)} async-done(((bf16[256,3072]{1,0:T(8,128)(2,1)}), bf16[1024,3072]{1,0:T(8,128)(2,1)}) %all-gather.9.cloned.1.call-update) | async-done | bytes 6291472 | tf_op jit(solution)/shard_map/all_gather | solution.py:86
  141.9 6.4 fusion.15
  148.3 4.9 copy.151
  153.2 7.4 %all-to-all-start.1 = ((bf16[2,1,256,3072]{3,0,1,2:T(2,128)(2,1)}), bf16[2,1,256,3072]{3,0,1,2:T(2,128)(2,1)}, u32[]{:S(2)}, u32[]{:S(2)}) async-start(bf16[2,1,256,3072]{3,0,1,2:T(2,128)(2,1)} %copy.151), calls=%async_computation.1 | async-start | bytes 6291456 | tf_op jit(solution)/shard_map/all_to_all | solution.py:103
  160.7 41.7 %all-gather.11.cloned.1.call-done = bf16[1024,1024]{1,0:T(8,128)(2,1)} async-done(((bf16[256,1024]{1,0:T(8,128)(2,1)}), bf16[1024,1024]{1,0:T(8,128)(2,1)}) %all-gather.11.cloned.1.call-update) | async-done | bytes 2097168 | tf_op jit(solution)/shard_map/all_gather | solution.py:87
  206.3 5.6 fusion.179
  223.5 4.8 fusion.182
  232.3 6.2 fusion.116
  238.4 5.9 fusion.119
  255.8 47.4 %all_to_all.19 = bf16[2,32,8,3072]{3,2,0,1:T(8,128)(2,1)S(1)} all-to-all(bf16[2,32,8,3072]{3,2,0,1:T(8,128)(2,1)S(1)} %copy.171), channel_id=1, replica_groups=mesh['frame'=32,'fsdp'=4] {'frame'}, dimensions={1} | all-to-all | bytes 6291456 | tf_op jit(solution)/shard_map/all_to_all | solution.py:115
  305.1 5.4 convolution_convert_fusion
  312.5 4.8 all-to-all-start
  322.6 10.5 %all-to-all-done = bf16[2,1,256,1024]{3,0,1,2:T(2,128)(2,1)} async-done(((bf16[2,1,256,1024]{3,0,1,2:T(2,128)(2,1)}), bf16[2,1,256,1024]{3,0,1,2:T(2,128)(2,1)}, u32[]{:S(2)}, u32[]{:S(2)}) %all-to-all-start) | async-done | bytes 1048608 | tf_op jit(solution)/shard_map/all_to_all | solution.py:102
  337.8 4.6 fusion.60
  342.5 7.7 %fusion.187 = (f32[512]{0:T(512)S(1)}, f32[512,1024]{1,0:T(8,128)}) fusion(bf16[512,3072]{1,0:T(8,128)(2,1)S(1)} %bitcast.178, bf16[1024,3072]{1,0:T(8,128)(2,1)} %all-gather.9.cloned.1.call-done), kind=kOutput, calls=%fused_computation.154 | convolution fusion | flops 3221749248 | bytes 11536384 | tf_op jit(solution)/shard_map/dot_general | solution.py:33
  352.7 4.7 fusion.88
  370.9 8.7 %fusion.107 = bf16[2,256,1,8,128]{1,4,3,0,2:T(8,128)(2,1)} fusion(bf16[2,256,8,128]{1,3,2,0:T(8,128)(2,1)} %bitcast.182, f32[2,8,256,256]{2,3,1,0:T(8,128)} %fusion.146, f32[2,8,256,256]{2,3,1,0:T(8,128)} %get-tuple-element.25, f32[2,8,256]{2,1,0:T(8,128)S(1)} %get-tuple-element.24), kind=kOutput, calls=%fused_computation.90 | convolution fusion | flops 276304128 | bytes 10502144 | tf_op jit(solution)/shard_map/bxhlm,blxhe->bmxhe/dot_general | solution.py:71
  382.0 8.7 %fusion.110 = bf16[2,256,1,8,128]{1,4,3,0,2:T(8,128)(2,1)} fusion(bf16[2,256,8,128]{1,3,2,0:T(8,128)(2,1)} %bitcast.180, f32[2,8,256,256]{2,3,1,0:T(8,128)} %fusion.146, f32[2,8,256,256]{2,3,1,0:T(8,128)} %get-tuple-element.25, f32[2,8,256]{2,1,0:T(8,128)S(1)} %get-tuple-element.24), kind=kOutput, calls=%fused_computation.91 | convolution fusion | flops 276304128 | bytes 10502144 | tf_op jit(solution)/shard_map/bxhlm,bmxhe->blxhe/dot_general | solution.py:70
  397.7 8.5 %fusion.188 = (f32[512]{0:T(512)S(1)}, f32[512,1024]{1,0:T(8,128)}) fusion(bf16[1024,3072]{1,0:T(8,128)(2,1)} %all-gather.5.cloned.1.call-done, bf16[512,1024]{1,0:T(8,128)(2,1)} %get-tuple-element.32, bf16[512,1024]{1,0:T(8,128)(2,1)} %get-tuple-element.33, bf16[512,1024]{1,0:T(8,128)(2,1)} %bitcast.184), kind=kOutput, calls=%fused_computation.155 | convolution fusion | flops 3231186432 | bytes 11536384 | tf_op jit(solution)/shard_map/dot_general | solution.py:33
  412.2 297.0 %all-reduce.2.cloned.1.call-done = bf16[256,3072]{1,0:T(8,128)(2,1)} async-done(((bf16[256,3072]{1,0:T(8,128)(2,1)}), bf16[256,3072]{1,0:T(8,128)(2,1)}) %all-reduce.2.cloned.1.call-update) | async-done | bytes 1572880 | tf_op jit(solution)/shard_map/psum | solution.py:131
  (100 shorter events, 95.0 us)
Async XLA Ops:
  7.2 2.8 copy-start
  7.2 55.6 %all-gather.5.cloned.1.call-start = ((), (), s32[]{:S(2)}) async-start(), calls=%async_computation.5 | async-start | bytes 7864320 | tf_op jit(solution)/shard_map/all_gather | solution.py:82
  7.9 82.5 %all-gather.7.cloned.1.call-start = ((), (), s32[]{:S(2)}) async-start(), calls=%async_computation.6 | async-start | bytes 2621440 | tf_op jit(solution)/shard_map/all_gather | solution.py:83
  8.7 133.2 %all-gather.9.cloned.1.call-start = ((), (), s32[]{:S(2)}) async-start(), calls=%async_computation.7 | async-start | bytes 7864320 | tf_op jit(solution)/shard_map/all_gather | solution.py:86
  9.4 193.0 %all-gather.11.cloned.1.call-start = ((), (), s32[]{:S(2)}) async-start(), calls=%async_computation.8 | async-start | bytes 2621440 | tf_op jit(solution)/shard_map/all_gather | solution.py:87
  70.9 9.1 %copy-start.2 = (bf16[64,8,8,128]{3,2,1,0:T(8,128)(2,1)}, bf16[64,8,8,128]{3,2,1,0:T(8,128)(2,1)S(1)}, u32[]{:S(2)}) copy-start(bf16[64,8,8,128]{3,2,1,0:T(8,128)(2,1)S(1)} %copy.205) | copy-start | bytes 3145732
  94.3 54.1 %copy-start.10 = (bf16[2,1,256,1024]{3,2,0,1:T(8,128)(2,1)}, bf16[2,1,256,1024]{3,2,0,1:T(8,128)(2,1)S(1)}, u32[]{:S(2)}) copy-start(bf16[2,1,256,1024]{3,2,0,1:T(8,128)(2,1)S(1)} %fusion.42) | copy-start | bytes 3145732
  153.2 49.2 %copy-start.9 = (bf16[2,32,8,1024]{3,2,1,0:T(8,128)(2,1)S(1)}, bf16[2,32,8,1024]{3,2,1,0:T(8,128)(2,1)}, u32[]{:S(2)}) copy-start(bf16[2,32,8,1024]{3,2,1,0:T(8,128)(2,1)} %param.11) | copy-start | bytes 3145732
  153.2 53.1 %all-to-all-start.1 = ((bf16[2,1,256,3072]{3,0,1,2:T(2,128)(2,1)}), bf16[2,1,256,3072]{3,0,1,2:T(2,128)(2,1)}, u32[]{:S(2)}, u32[]{:S(2)}) async-start(bf16[2,1,256,3072]{3,0,1,2:T(2,128)(2,1)} %copy.151), calls=%async_computation.1 | async-start | bytes 6291456 | tf_op jit(solution)/shard_map/all_to_all | solution.py:103
  160.7 237.1 %reduce-scatter.2.cloned.1.call-start = ((), (), s32[]{:S(2)}) async-start(), calls=%async_computation.9 | async-start | bytes 7864320 | tf_op jit(solution)/shard_map/reduce_scatter | solution.py:123
  213.7 5.5 copy-start.3
  223.5 4.8 copy-start.13
  232.3 6.2 copy-start.12
  303.2 1.9 copy-start.11
  303.4 1.7 copy-start.7
  312.5 7.4 %copy-start.4 = (bf16[2,32,8,8,128]{4,3,0,2,1:T(8,128)(2,1)S(1)}, bf16[2,32,8,8,128]{4,3,0,2,1:T(8,128)(2,1)}, u32[]{:S(2)}) copy-start(bf16[2,32,8,8,128]{4,3,0,2,1:T(8,128)(2,1)} %copy-done.3) | copy-start | bytes 3145732
  312.5 20.6 %all-to-all-start = ((bf16[2,1,256,1024]{3,0,1,2:T(2,128)(2,1)}), bf16[2,1,256,1024]{3,0,1,2:T(2,128)(2,1)}, u32[]{:S(2)}, u32[]{:S(2)}) async-start(bf16[2,1,256,1024]{3,0,1,2:T(2,128)(2,1)} %copy.149), calls=%async_computation | async-start | bytes 2097152 | tf_op jit(solution)/shard_map/all_to_all | solution.py:102
  317.4 2.6 copy-start.14
  333.2 19.5 %all-to-all-start.2 = ((bf16[2,32,8,1024]{3,2,0,1:T(8,128)(2,1)}), bf16[2,32,8,1024]{3,2,0,1:T(8,128)(2,1)S(1)}, u32[]{:S(2)}, u32[]{:S(2)}) async-start(bf16[2,32,8,1024]{3,2,0,1:T(8,128)(2,1)} %copy.160), calls=%async_computation.2 | async-start | bytes 2097152 | tf_op jit(solution)/shard_map/all_to_all | solution.py:116
  337.8 371.4 %all-reduce.2.cloned.1.call-start = ((), (), s32[]{:S(2)}) async-start(), calls=%async_computation.10 | async-start | bytes 3145728 | tf_op jit(solution)/shard_map/psum | solution.py:131
  337.8 4.7 copy-start.8
  393.2 2.6 copy-start.5
  393.2 2.6 copy-start.6
  406.3 2.3 copy-start.1
Sparse Core Ops, SparseCore 0:
  9.7 53.0 all-gather.4
  64.4 25.9 all-gather.6
  92.1 49.7 all-gather.8
  143.4 58.9 all-gather.10
  310.6 74.0 reduce-scatter.1
  397.9 311.3 all-reduce.1
where the time goes:
time: 730 us; the launch traced here: 720 us
  waiting for transfers between devices  460 us (63%)
  matrix products  111 us (15%)
  local copies, waits for them, and re-layouts  55.2 us (8%)
  blocking collectives  47.4 us (6%)
  starting transfers between devices  17.1 us (2%)
  other arithmetic  15 us (2%)
  between operations  14.5 us (2%)
    psum x1, waiting for transfers between devices, body(): grad_tm_qkv = lax.psum(shard, 'frame').astype(jnp.float32)  297 us
    all_gather x1, waiting for transfers between devices, body(): lax.all_gather(sp_qkv, 'fsdp', axis=0, tiled=True)  52.1 us
    all_gather x1, waiting for transfers between devices, body(): lax.all_gather(tm_qkv, 'fsdp', axis=0, tiled=True)  47.6 us
    all_to_all x1, blocking collectives, body(): lax.all_to_all(d_qkv_pos, 'frame', split_axis=1, concat_axis=2, tiled=True)  47.4 us
    all_gather x1, waiting for transfers between devices, body(): lax.all_gather(tm_out, 'fsdp', axis=0, tiled=True)  41.7 us
    dot_general x4, matrix products, times_t(): lax.dot_general(flat, weight, (((1,), (1,)), ((), ())), preferred_element...  24.8 us
    dot_general x4, matrix products, times(): prod = jnp.dot(flat, weight, preferred_element_type=jnp.float32)  20.5 us
    dot_general x2, matrix products, attend_back(): jnp.einsum('bxhlm,blxhe->bmxhe', d_low, query, preferred_element_type=jnp...  14.9 us
  transfers between devices with their start and end apart: 9, of which 7 were waited for; matrix products, arithmetic and copies ran while one was open for 17% of the time, Pallas kernels for 0%

commit v1 on v0

--- a/solution.py
+++ b/solution.py
@@ -76,16 +76,16 @@
     return jnp.concatenate([p.reshape(shape) for p in parts], axis=-1).astype(jnp.bfloat16)
 
 
+def gather_rows(shard):
+    rows = shard.shape[0] // lax.axis_size("frame")
+    mine = lax.dynamic_slice_in_dim(shard, lax.axis_index("frame") * rows, rows, 0)
+    return lax.all_gather(mine, ("fsdp", "frame"), axis=0, tiled=True)
+
+
 def body(frames_in, sp_qkv, sp_out, tm_qkv, tm_out, cotangent):
     clips, frames_local, tokens_frame, width = frames_in.shape
-    sp_qkv_all, sp_out_all = (
-        lax.all_gather(sp_qkv, "fsdp", axis=0, tiled=True),
-        lax.all_gather(sp_out, "fsdp", axis=0, tiled=True),
-    )
-    tm_qkv_all, tm_out_all = (
-        lax.all_gather(tm_qkv, "fsdp", axis=0, tiled=True),
-        lax.all_gather(tm_out, "fsdp", axis=0, tiled=True),
-    )
+    sp_qkv_all, sp_out_all = (gather_rows(sp_qkv), gather_rows(sp_out))
+    tm_qkv_all, tm_out_all = (gather_rows(tm_qkv), gather_rows(tm_out))
     normed_one, rstd_one = normalize(frames_in.astype(jnp.float32))
     spatial_qkv = times(normed_one.astype(jnp.bfloat16), sp_qkv_all).astype(jnp.bfloat16)
     sq, sk, sv = split_heads(
@@ -94,14 +94,10 @@
     spatial_att, sp_probs, sp_low = attend(sq, sk, sv, False)
     spatial_att = spatial_att.reshape(frames_in.shape)
     stream = (frames_in.astype(jnp.float32) + times(spatial_att, sp_out_all)).astype(jnp.bfloat16)
-    stream = lax.optimization_barrier(stream)
-    normed_two, rstd_two = normalize(stream.astype(jnp.float32))
+    stream_pos = lax.all_to_all(stream, "frame", split_axis=2, concat_axis=1, tiled=True)
+    normed_two, rstd_two = normalize(stream_pos.astype(jnp.float32))
     low_two = normed_two.astype(jnp.bfloat16)
-    temporal_qkv = times(low_two, tm_qkv_all).astype(jnp.bfloat16)
-    stream_pos, qkv_pos = (
-        lax.all_to_all(stream, "frame", split_axis=2, concat_axis=1, tiled=True),
-        lax.all_to_all(temporal_qkv, "frame", split_axis=2, concat_axis=1, tiled=True),
-    )
+    qkv_pos = times(low_two, tm_qkv_all).astype(jnp.bfloat16)
     tq, tk, tv = split_heads(qkv_pos, HEADS)
     temporal_att, tm_probs, tm_low = attend(tq, tk, tv, True)
     temporal_att = temporal_att.reshape(stream_pos.shape)
@@ -111,25 +107,25 @@
     d_temporal_att = times_t(cotangent, tm_out_all).astype(jnp.bfloat16)
     parts = attend_back(tq, tk, tv, tm_probs, tm_low, d_temporal_att.reshape(tq.shape))
     d_qkv_pos = join_heads(parts, stream_pos.shape)
-    d_qkv_frame, cot_frame = (
-        lax.all_to_all(d_qkv_pos, "frame", split_axis=1, concat_axis=2, tiled=True),
-        lax.all_to_all(cotangent, "frame", split_axis=1, concat_axis=2, tiled=True),
+    d_stream_pos = cotangent.astype(jnp.float32) + norm_back(
+        normed_two, rstd_two, times_t(d_qkv_pos, tm_qkv_all)
     )
-    d_stream = cot_frame.astype(jnp.float32) + norm_back(
-        normed_two, rstd_two, times_t(d_qkv_frame, tm_qkv_all)
+    d_stream_low = lax.all_to_all(
+        d_stream_pos.astype(jnp.bfloat16), "frame", split_axis=1, concat_axis=2, tiled=True
     )
+    d_stream = d_stream_low.astype(jnp.float32)
     left_rows = low_two.reshape(-1, width)
-    right_rows = d_qkv_frame.reshape(-1, 3 * width)
-    shard = lax.psum_scatter(
+    right_rows = d_qkv_pos.reshape(-1, 3 * width)
+    piece = lax.psum_scatter(
         lax.dot_general(
             left_rows, right_rows, (((0,), (0,)), ((), ())), preferred_element_type=jnp.float32
         ).astype(jnp.bfloat16),
-        "fsdp",
+        ("fsdp", "frame"),
         scatter_dimension=0,
         tiled=True,
     )
-    grad_tm_qkv = lax.psum(shard, "frame").astype(jnp.float32)
-    d_spatial_att = times_t(d_stream.astype(jnp.bfloat16), sp_out_all).astype(jnp.bfloat16)
+    grad_tm_qkv = lax.all_gather(piece, "frame", axis=0, tiled=True).astype(jnp.float32)
+    d_spatial_att = times_t(d_stream_low, sp_out_all).astype(jnp.bfloat16)
     parts = attend_back(sq, sk, sv, sp_probs, sp_low, d_spatial_att.reshape(sq.shape))
     d_spatial_qkv = join_heads(parts, frames_in.shape)
     grad_in = d_stream + norm_back(normed_one, rstd_one, times_t(d_spatial_qkv, sp_qkv_all))

time: 730 us -> 2120 us (2.90)
  waiting for transfers between devices: 460 us -> 1910 us
  blocking collectives: 47.4 us -> 0 us
    all_gather x4 -> x5, waiting for transfers between devices: 149 us -> 1290 us  [the longest x4 1180 us: gather_rows(): return lax.all_gather(mine, ('fsdp', 'frame'), axis=0, tiled=True)]
    reduce_scatter x1, waiting for transfers between devices: 0.01 us -> 612 us  [body(): lax.psum_scatter(lax.dot_general(left_rows, right_rows, (((0,), (0,)), ((...]
    psum x1 -> x0, waiting for transfers between devices: 297 us -> none  [body(): grad_tm_qkv = lax.psum(shard, 'frame').astype(jnp.float32)]
    all_to_all x1 -> x0, blocking collectives: 47.4 us -> none  [body(): lax.all_to_all(d_qkv_pos, 'frame', split_axis=1, concat_axis=2, tiled=True)]
  transfers between devices with their start and end apart: 9 -> 8, of which waited for: 7 -> 7; matrix products, arithmetic and copies ran while one was open for 17% -> 5% of each run, Pallas kernels for 0% -> 0%
where the time goes in v1:
time: 2120 us; the launch traced here: 2110 us
  waiting for transfers between devices  1910 us (90%)
  matrix products  107 us (5%)
  local copies, waits for them, and re-layouts  46.6 us (2%)
    all_gather x4, waiting for transfers between devices, gather_rows(): return lax.all_gather(mine, ('fsdp', 'frame'), axis=0, tiled=True)  1180 us
    reduce_scatter x1, waiting for transfers between devices, body(): lax.psum_scatter(lax.dot_general(left_rows, right_rows, (((0,), (0,)), ((...  612 us
    all_gather x1, waiting for transfers between devices, body(): lax.all_gather(piece, 'frame', axis=0, tiled=True).astype(jnp.float32)  106 us
  transfers between devices with their start and end apart: 8, of which 7 were waited for; matrix products, arithmetic and copies ran while one was open for 5% of the time, Pallas kernels for 0%

profile of v1, /device:TPU:0, one launch (start us, length us, event | category | flops | bytes accessed | tf_op | source)
XLA Modules:
  0.0 2108.2 jit_solution(4730118461941708513)
XLA Ops:
  15.4 308.0 %all-gather.6.cloned.1.call-done = bf16[1024,3072]{1,0:T(8,128)(2,1)} async-done(((bf16[8,3072]{1,0:T(8,128)(2,1)}), bf16[1024,3072]{1,0:T(8,128)(2,1)}) %all-gather.6.cloned.1.call-update) | async-done | bytes 6291472 | tf_op jit(solution)/shard_map/all_gather | solution.py:82
  323.4 6.6 fusion.17
  336.7 5.5 fusion.165
  342.3 3.8 convolution_convert_fusion.4
  346.0 281.2 %all-gather.8.cloned.1.call-done = bf16[1024,1024]{1,0:T(8,128)(2,1)} async-done(((bf16[8,1024]{1,0:T(8,128)(2,1)}), bf16[1024,1024]{1,0:T(8,128)(2,1)}) %all-gather.8.cloned.1.call-update) | async-done | bytes 2097168 | tf_op jit(solution)/shard_map/all_gather | solution.py:82
  632.5 7.9 all-to-all-start
  641.0 285.5 %all-gather.12.cloned.1.call-done = bf16[1024,1024]{1,0:T(8,128)(2,1)} async-done(((bf16[8,1024]{1,0:T(8,128)(2,1)}), bf16[1024,1024]{1,0:T(8,128)(2,1)}) %all-gather.12.cloned.1.call-update) | async-done | bytes 2097168 | tf_op jit(solution)/shard_map/all_gather | solution.py:82
  935.2 304.8 %all-gather.10.cloned.1.call-done = bf16[1024,3072]{1,0:T(8,128)(2,1)} async-done(((bf16[8,3072]{1,0:T(8,128)(2,1)}), bf16[1024,3072]{1,0:T(8,128)(2,1)}) %all-gather.10.cloned.1.call-update) | async-done | bytes 6291472 | tf_op jit(solution)/shard_map/all_gather | solution.py:82
  1240.0 6.8 fusion.13
  1252.0 5.7 fusion.166
  1257.7 6.6 fusion.102
  1264.3 6.4 fusion.99
  1270.7 3.5 fusion.92
  1290.4 6.3 bitcast_convert_fusion
  1296.8 7.1 fusion.163
  1306.2 8.4 all-to-all-start.1
  1319.5 4.5 fusion.52
  1324.0 9.2 all-to-all-done.1
  1337.0 612.0 %reduce-scatter.2.cloned.1.call-done = bf16[8,3072]{1,0:T(8,128)(2,1)} async-done(((bf16[1024,3072]{1,0:T(8,128)(2,1)}), bf16[8,3072]{1,0:T(8,128)(2,1)}) %reduce-scatter.2.cloned.1.call-update) | async-done | bytes 49168 | tf_op jit(solution)/shard_map/reduce_scatter | solution.py:119
  1949.0 4.0 fusion.91
  1958.8 7.4 fusion.93
  1968.3 7.4 fusion.96
  1978.2 7.6 fusion.171
  1991.6 105.8 %all-gather.14.cloned.1.call-done = bf16[256,3072]{1,0:T(8,128)(2,1)} async-done(((bf16[8,3072]{1,0:T(8,128)(2,1)}), bf16[256,3072]{1,0:T(8,128)(2,1)}) %all-gather.14.cloned.1.call-update) | async-done | bytes 1572880 | tf_op jit(solution)/shard_map/all_gather | solution.py:127
  (121 shorter events, 81.2 us)
Async XLA Ops:
  7.2 7.8 copy-start.2
  7.2 316.2 %all-gather.6.cloned.1.call-start = ((), (), s32[]{:S(2)}) async-start(), calls=%async_computation.3 | async-start | bytes 6340608 | tf_op jit(solution)/shard_map/all_gather | solution.py:82
  9.2 618.0 %all-gather.8.cloned.1.call-start = ((), (), s32[]{:S(2)}) async-start(), calls=%async_computation.4 | async-start | bytes 2113536 | tf_op jit(solution)/shard_map/all_gather | solution.py:82
  10.6 915.8 %all-gather.12.cloned.1.call-start = ((), (), s32[]{:S(2)}) async-start(), calls=%async_computation.6 | async-start | bytes 2113536 | tf_op jit(solution)/shard_map/all_gather | solution.py:82
  12.0 1228.0 %all-gather.10.cloned.1.call-start = ((), (), s32[]{:S(2)}) async-start(), calls=%async_computation.5 | async-start | bytes 6340608 | tf_op jit(solution)/shard_map/all_gather | solution.py:82
  15.0 308.4 %copy-start.19 = (f32[2,256]{1,0:T(2,128)}, f32[2,256]{1,0:T(2,128)S(1)}, u32[]{:S(2)}) copy-start(f32[2,256]{1,0:T(2,128)S(1)} %broadcast_multiply_fusion.5) | copy-start | bytes 6148
  15.4 308.0 %copy-start.21 = (f32[2,256]{1,0:T(2,128)}, f32[2,256]{1,0:T(2,128)S(1)}, u32[]{:S(2)}) copy-start(f32[2,256]{1,0:T(2,128)S(1)} %add_rsqrt_fusion.1) | copy-start | bytes 6148
  336.7 5.5 copy-start.6
  342.3 3.8 copy-start.23
  630.4 296.1 %copy-start.11 = (bf16[2,32,8,1024]{3,2,1,0:T(8,128)(2,1)S(1)}, bf16[2,32,8,1024]{3,2,1,0:T(8,128)(2,1)}, u32[]{:S(2)}) copy-start(bf16[2,32,8,1024]{3,2,1,0:T(8,128)(2,1)} %param.11) | copy-start | bytes 3145732
  632.5 298.7 %all-to-all-start = ((bf16[2,1,256,1024]{3,0,1,2:T(2,128)(2,1)}), bf16[2,1,256,1024]{3,0,1,2:T(2,128)(2,1)S(1)}, u32[]{:S(2)}, u32[]{:S(2)}) async-start(bf16[2,1,256,1024]{3,0,1,2:T(2,128)(2,1)} %copy.159), calls=%async_computation | async-start | bytes 2097152 | tf_op jit(solution)/shard_map/all_to_all | solution.py:97
  640.4 1308.6 %reduce-scatter.2.cloned.1.call-start = ((), (), s32[]{:S(2)}) async-start(), calls=%async_computation.7 | async-start | bytes 6340608 | tf_op jit(solution)/shard_map/reduce_scatter | solution.py:119
  1248.9 3.2 copy-start.9
  1270.7 3.5 copy-start.17
  1296.8 7.2 copy-start.12
  1305.1 9.5 copy-start.10
  1306.2 27.0 %all-to-all-start.1 = ((bf16[2,32,8,1024]{3,2,0,1:T(8,128)(2,1)}), bf16[2,32,8,1024]{3,2,0,1:T(8,128)(2,1)}, u32[]{:S(2)}, u32[]{:S(2)}) async-start(bf16[2,32,8,1024]{3,2,0,1:T(8,128)(2,1)} %copy.179), calls=%async_computation.1 | async-start | bytes 2097152 | tf_op jit(solution)/shard_map/all_to_all | solution.py:113
  1314.5 782.8 %all-gather.14.cloned.1.call-start = ((), (), s32[]{:S(2)}) async-start(), calls=%async_computation.8 | async-start | bytes 1622016 | tf_op jit(solution)/shard_map/all_gather | solution.py:127
  1336.4 612.6 %copy-start.24 = (f32[2,8,256]{2,1,0:T(8,128)S(1)}, f32[2,8,256]{2,1,0:T(8,128)}, u32[]{:S(2)}) copy-start(f32[2,8,256]{2,1,0:T(8,128)} %copy-done.23) | copy-start | bytes 49156
  1953.0 3.1 copy-start.7
  1978.2 7.7 copy-start.3
  1978.2 7.7 copy-start.20
  1978.2 7.7 copy-start.22
  1988.2 112.6 %copy-start.1 = (bf16[256,3072]{1,0:T(8,128)(2,1)S(1)}, bf16[256,3072]{1,0:T(8,128)(2,1)}, u32[]{:S(2)}) copy-start(bf16[256,3072]{1,0:T(8,128)(2,1)} %param.7) | copy-start | bytes 4718596
  (9 other events, 16.4 us)
Sparse Core Ops, SparseCore 0:
  10.3 313.0 all-gather.5
  325.1 302.0 all-gather.7
  628.9 297.4 all-gather.11
  928.6 311.4 all-gather.9
  1296.9 652.0 reduce-scatter.1
  1950.6 146.7 all-gather.13

commit v2 on v1

v2 whole, which is shorter than its diff:
```python
import functools

import jax
import jax.numpy as jnp
from jax import lax
from jax.experimental import pallas as pl
from jax.experimental.pallas import tpu as pltpu
from jax.sharding import PartitionSpec as P

MESH = pl.DeviceIdType.MESH
F32 = jnp.float32
BF16 = jnp.bfloat16
EPS = 1e-05
HEADS = 8
HEAD = 128
SCALE = HEAD**-0.5
D = 1024
T = 512
CLIP = 256
VMEM_LIMIT = 60 * 1024 * 1024


def dot(left, right):
    return lax.dot_general(left, right, (((1,), (0,)), ((), ())), preferred_element_type=F32)


def dot_nt(left, right):
    return lax.dot_general(left, right, (((1,), (1,)), ((), ())), preferred_element_type=F32)


def dot_tn(left, right):
    return lax.dot_general(left, right, (((0,), (0,)), ((), ())), preferred_element_type=F32)


def ds(index, size):
    return pl.ds(pl.multiple_of(index * size, size), size)


def loop(count, unroll=1):
    def run(body):
        def step(i, carry):
            body(i)
            return carry

        lax.fori_loop(0, count, step, 0, unroll=unroll)

    return run


def normalize(u):
    mean = jnp.mean(u, axis=-1, keepdims=True)
    cent = u - mean
    rstd = lax.rsqrt(jnp.mean(cent * cent, axis=-1, keepdims=True) + EPS)
    return cent * rstd, rstd


def norm_back(normed, rstd, grad):
    first = jnp.mean(grad, axis=-1, keepdims=True)
    second = jnp.mean(grad * normed, axis=-1, keepdims=True)
    return rstd * (grad - first - normed * second)


def softmax(scores):
    top = jnp.max(scores, axis=-1, keepdims=True)
    expo = jnp.exp(scores - top)
    return expo / jnp.sum(expo, axis=-1, keepdims=True)


def attend_back(q, k, v, probs, low, a):
    d_probs = dot_nt(a, v)
    d_v = dot_tn(low, a)
    prod = d_probs * probs
    d_s = ((prod - probs * jnp.sum(prod, axis=-1, keepdims=True)) * SCALE).astype(BF16)
    return dot(d_s, k), dot_tn(d_s, q), d_v


def part(i, head):
    return pl.ds(pl.multiple_of((i * HEADS + head) * HEAD, HEAD), HEAD)


def to_chunks(rows):
    parts = []
    for d in range(32):
        parts.append(rows[8 * d : 8 * d + 8])
        parts.append(rows[CLIP + 8 * d : CLIP + 8 * d + 8])
    return jnp.concatenate(parts, axis=0)


def from_chunks(rows):
    return jnp.concatenate(
        [rows[16 * d + 8 * c : 16 * d + 8 * c + 8] for c in range(2) for d in range(32)], axis=0
    )


def spatial_kernel(x_ref, wqkv_ref, wo_ref, qkv_ref, stream_ref, nrm, att):
    @loop(8)
    def _(r):
        rows = ds(r, 64)
        nrm[rows, :] = normalize(x_ref[rows, :].astype(F32))[0].astype(BF16)

    @loop(6)
    def _(n):
        cols = ds(n, 512)
        qkv_ref[:, cols] = dot(nrm[...], wqkv_ref[:, cols]).astype(BF16)

    @loop(8)
    def _(h):
        for c in range(2):
            rows = pl.ds(c * CLIP, CLIP)
            q, k, v = (qkv_ref[rows, part(i, h)] for i in range(3))
            low = softmax(dot_nt(q, k) * SCALE).astype(BF16)
            att[rows, part(0, h)] = dot(low, v).astype(BF16)

    @loop(4)
    def _(n):
        cols = ds(n, 256)
        out = dot(att[...], wo_ref[:, cols]) + x_ref[:, cols].astype(F32)
        stream_ref[:, cols] = to_chunks(out).astype(BF16)


def temporal_kernel(
    s_ref, cot_ref, wqkv_ref, wo_ref, out_ref, dchunk_ref, low_ref, dqkv_ref,
    stream, qkv, da, att, bias, grad,
):
    @loop(8)
    def _(n):
        cols = ds(n, 128)
        stream[:, cols] = from_chunks(s_ref[:, cols].astype(F32)).astype(BF16)

    @loop(8)
    def _(r):
        rows = ds(r, 64)
        low_ref[rows, :] = normalize(stream[rows, :].astype(F32))[0].astype(BF16)

    @loop(6)
    def _(n):
        cols = ds(n, 512)
        qkv[:, cols] = dot(low_ref[...], wqkv_ref[:, cols]).astype(BF16)

    @loop(2)
    def _(n):
        cols = ds(n, 512)
        da[:, cols] = dot_nt(cot_ref[...], wo_ref[cols, :]).astype(BF16)

    row = lax.broadcasted_iota(jnp.int32, (CLIP, CLIP), 0)
    col = lax.broadcasted_iota(jnp.int32, (CLIP, CLIP), 1)
    allowed = (col <= row) & (((row - col) & 7) == 0)
    bias[...] = jnp.where(allowed, 0.0, -1e30)

    @loop(8)
    def _(h):
        for c in range(2):
            rows = pl.ds(c * CLIP, CLIP)
            q, k, v = (qkv[rows, part(i, h)] for i in range(3))
            probs = softmax(dot_nt(q, k) * SCALE + bias[...])
            low = probs.astype(BF16)
            att[rows, part(0, h)] = dot(low, v).astype(BF16)
            parts = attend_back(q, k, v, probs, low, da[rows, part(0, h)])
            for i in range(3):
                dqkv_ref[rows, part(i, h)] = parts[i].astype(BF16)

    @loop(2)
    def _(n):
        cols = ds(n, 512)
        out = dot(att[...], wo_ref[:, cols]) + stream[:, cols].astype(F32)
        out_ref[:, cols] = out.astype(BF16)

    @loop(4)
    def _(n):
        cols = ds(n, 256)
        grad[:, cols] = dot_nt(dqkv_ref[...], wqkv_ref[cols, :])

    @loop(8)
    def _(r):
        rows = ds(r, 64)
        normed, rstd = normalize(stream[rows, :].astype(F32))
        grad[rows, :] = cot_ref[rows, :].astype(F32) + norm_back(normed, rstd, grad[rows, :])

    @loop(8)
    def _(n):
        cols = ds(n, 128)
        dchunk_ref[:, cols] = to_chunks(grad[:, cols]).astype(BF16)


def spatial_back_kernel(x_ref, d_ref, qkv_ref, wqkv_ref, wo_ref, out_ref, dstr, da, dqkv):
    @loop(8)
    def _(n):
        cols = ds(n, 128)
        dstr[:, cols] = from_chunks(d_ref[:, cols].astype(F32)).astype(BF16)

    @loop(2)
    def _(n):
        cols = ds(n, 512)
        da[:, cols] = dot_nt(dstr[...], wo_ref[cols, :]).astype(BF16)

    @loop(8)
    def _(h):
        for c in range(2):
            rows = pl.ds(c * CLIP, CLIP)
            q, k, v = (qkv_ref[rows, part(i, h)] for i in range(3))
            probs = softmax(dot_nt(q, k) * SCALE)
            parts = attend_back(q, k, v, probs, probs.astype(BF16), da[rows, part(0, h)])
            for i in range(3):
                dqkv[rows, part(i, h)] = parts[i].astype(BF16)

    @loop(4)
    def _(n):
        cols = ds(n, 256)
        out_ref[:, cols] = dot_nt(dqkv[...], wqkv_ref[cols, :])

    @loop(8)
    def _(r):
        rows = ds(r, 64)
        normed, rstd = normalize(x_ref[rows, :].astype(F32))
        out_ref[rows, :] = dstr[rows, :].astype(F32) + norm_back(normed, rstd, out_ref[rows, :])


class Place:
    def __init__(self):
        frame, fsdp = lax.axis_index("frame"), lax.axis_index("fsdp")
        self.lo, x, y = lax.div(frame, 16), lax.rem(lax.div(frame, 4), 4), lax.rem(frame, 4)
        self.hi, self.core = lax.div(fsdp, 2), lax.rem(fsdp, 2)
        self.x, self.y = x, y
        self.a = x + self.core * (y - x)
        self.b = y + self.core * (x - y)
        self.ap, self.am = lax.rem(self.a + 1, 4), lax.rem(self.a + 3, 4)
        self.bp, self.bm = lax.rem(self.b + 1, 4), lax.rem(self.b + 3, 4)
        self.a2, self.b2 = lax.rem(self.a + 2, 4), lax.rem(self.b + 2, 4)
        self.fsdp = fsdp
        self.sibling = (frame, self.hi * 2 + 1 - self.core)
        self.cross = ((1 - self.lo) * 16 + x * 4 + y, (1 - self.hi) * 2 + self.core)
        self.twin = ((1 - self.lo) * 16 + x * 4 + y, fsdp)
        self.a_next, self.a_prev = self.at(self.ap, self.b), self.at(self.am, self.b)
        self.b_next, self.b_prev = self.at(self.a, self.bp), self.at(self.a, self.bm)

    def at(self, a, b):
        x = a + self.core * (b - a)
        y = b + self.core * (a - b)
        return (self.lo * 16 + x * 4 + y, self.fsdp)


def greet(devices):
    barrier = pltpu.get_barrier_semaphore()
    for device in devices:
        pl.semaphore_signal(barrier, inc=1, device_id=device, device_id_type=MESH)
    pl.semaphore_wait(barrier, len(devices))


class Copies:
    def __init__(self, send, recv):
        self.send, self.recv, self.count, self.started = send, recv, 0, []

    def start(self, src, dst, device):
        i = self.count
        self.count += 1
        copy = pltpu.make_async_remote_copy(
            src_ref=src, dst_ref=dst, send_sem=self.send.at[i], recv_sem=self.recv.at[i],
            device_id=device, device_id_type=MESH,
        )
        copy.start()
        self.started.append(copy)
        return copy

    def finish(self):
        for copy in self.started:
            copy.wait_send()


def rows_at(index, size):
    return pl.ds(pl.multiple_of(index, size), size)


def gather_steps(copies, here, shard, out):
    width = shard.shape[1]
    half = width // 2
    lo, hi = pl.ds(0, half), pl.ds(half, half)
    own = here.fsdp * 256
    base = ((1 - here.hi) * 2 + here.core) * 256

    piece = (here.b * 4 + here.a) * 16
    cross = copies.start(shard.at[rows_at(piece, 16), :], out.at[rows_at(own + piece, 16), :], here.cross)
    mine = copies.start(shard, out.at[rows_at(own, 256), :], here.sibling)
    yield
    cross.wait_recv()

    def spread(size, offset, here_at, before, after, nxt, prv):
        def rows(i):
            return rows_at(base + offset + i * size, size)

        block = out.at[rows(here_at), :]
        right = copies.start(block, block, nxt)
        left = copies.start(block, block, prv)
        yield
        right.wait_recv()
        ahead = out.at[rows(before), lo]
        right2 = copies.start(ahead, ahead, nxt)
        left.wait_recv()
        ahead = out.at[rows(after), hi]
        left2 = copies.start(ahead, ahead, prv)
        yield
        right2.wait_recv()
        left2.wait_recv()

    yield from spread(16, here.b * 64, here.a, here.am, here.ap, here.a_next, here.a_prev)

    def over(i):
        block = out.at[rows_at(base + i * 64, 64), :]
        return copies.start(block, block, here.sibling)

    spreading = spread(64, 0, here.b, here.bm, here.bp, here.b_next, here.b_prev)
    next(spreading)
    last = [over(here.b)]
    yield
    next(spreading)
    last += [over(here.bm), over(here.bp)]
    yield
    for _ in spreading:
        pass
    last.append(over(here.b2))
    yield
    mine.wait_recv()
    for copy in last:
        copy.wait_recv()


GATHER_COPIES = 14


def gather_kernel(*refs):
    shards, outs, (send, recv, local) = refs[:4], refs[4:8], refs[8:]
    here = Place()
    greet([here.sibling, here.cross, here.a_next, here.a_prev, here.b_next, here.b_prev])
    copies = Copies(send, recv)
    locals_ = []
    for i in range(4):
        copy = pltpu.make_async_copy(
            shards[i], outs[i].at[rows_at(here.fsdp * 256, 256), :], local.at[i]
        )
        locals_.append(copy)
    waiting = [gather_steps(copies, here, shards[i], outs[i]) for i in range(4)]
    for steps in waiting:
        next(steps)
    for copy in locals_:
        copy.start()
    while waiting:
        for steps in list(waiting):
            try:
                next(steps)
            except StopIteration:
                waiting.remove(steps)
    copies.finish()
    for copy in locals_:
        copy.wait()


def reduce_kernel(low_ref, dq_ref, out_ref, give, take, held, rb1, rb2, ra1, ra2, piece, rz, total, send, recv):
    here = Place()
    greet([here.sibling, here.cross, here.twin, here.a_next, here.a_prev, here.b_next, here.b_prev])
    copies = Copies(send, recv)
    half = 3 * D // 2
    lo, hi = pl.ds(0, half), pl.ds(half, half)

    def left(h, core):
        return low_ref[:, rows_at((h * 2 + core) * 256, 256)]

    siblings = []
    for h in range(2):

        @loop(6)
        def _(n):
            cols = ds(n, 512)
            give[h, :, cols] = dot_tn(left(h, 1 - here.core), dq_ref[:, cols]).astype(BF16)

        siblings.append(copies.start(give.at[h], take.at[h], here.sibling))
    for h in range(2):
        siblings[h].wait_recv()

        @loop(6)
        def _(n):
            cols = ds(n, 512)
            held[h, :, cols] = (
                dot_tn(left(h, here.core), dq_ref[:, cols]) + take[h, :, cols].astype(F32)
            ).astype(BF16)

    def add(rows, cols, *others):
        total_ = held[:, rows, cols].astype(F32)
        for other in others:
            total_ = total_ + other.astype(F32)
        held[:, rows, cols] = total_.astype(BF16)

    def scatter(size, offset, at, before, after, opposite, nxt, prv, first, second):
        def rows(i):
            return rows_at(offset + i * size, size)

        def send_(i, cols, dst, device):
            return copies.start(held.at[:, rows(i), cols], dst, device)

        one = send_(opposite, lo, first.at[:, :, lo], nxt)
        two = send_(opposite, hi, first.at[:, :, hi], prv)
        three = send_(after, hi, second.at[0, :, :, hi], nxt)
        four = send_(before, lo, second.at[1, :, :, lo], prv)
        one.wait_recv()
        add(rows(after), lo, first[:, :, lo])
        five = send_(after, lo, second.at[0, :, :, lo], nxt)
        two.wait_recv()
        add(rows(before), hi, first[:, :, hi])
        six = send_(before, hi, second.at[1, :, :, hi], prv)
        for copy in (three, four, five, six):
            copy.wait_recv()
        add(rows(at), slice(None), second[0], second[1])

    scatter(64, 0, here.b, here.bm, here.bp, here.b2, here.b_next, here.b_prev, rb1, rb2)
    base = here.b * 64
    scatter(16, base, here.a, here.am, here.ap, here.a2, here.a_next, here.a_prev, ra1, ra2)

    mine = rows_at(base + here.a * 16, 16)
    cross = copies.start(held.at[1 - here.hi, mine, :], rz.at[0], here.cross)
    cross.wait_recv()
    piece[...] = (held[here.hi, mine, :].astype(F32) + rz[0].astype(F32)).astype(BF16)
    twin = copies.start(piece, rz.at[1], here.twin)
    twin.wait_recv()
    total[mine, :] = (piece[...].astype(F32) + rz[1].astype(F32)).astype(BF16)

    def spread(size, offset, at, before, after, nxt, prv):
        def rows(i):
            return rows_at(offset + i * size, size)

        block = total.at[rows(at), :]
        right = copies.start(block, block, nxt)
        left_ = copies.start(block, block, prv)
        right.wait_recv()
        ahead = total.at[rows(before), lo]
        right2 = copies.start(ahead, ahead, nxt)
        left_.wait_recv()
        ahead = total.at[rows(after), hi]
        left2 = copies.start(ahead, ahead, prv)
        right2.wait_recv()
        left2.wait_recv()

    spread(16, base, here.a, here.am, here.ap, here.a_next, here.a_prev)
    spread(64, 0, here.b, here.bm, here.bp, here.b_next, here.b_prev)
    out_ref[...] = total[...].astype(F32)
    copies.finish()


REDUCE_COPIES = 24
VM = pl.BlockSpec(memory_space=pltpu.VMEM)
ANY = pl.BlockSpec(memory_space=pl.ANY)


def sds(shape, dtype):
    return jax.ShapeDtypeStruct(shape, dtype)


def call(kernel, ins, outs, scratch, collective=None, specs=None, out_specs=None):
    extra = {} if collective is None else dict(collective_id=collective, has_side_effects=True)
    return pl.pallas_call(
        kernel,
        out_shape=outs,
        in_specs=specs or [VM] * len(ins),
        out_specs=out_specs or [VM] * len(outs),
        scratch_shapes=scratch,
        compiler_params=pltpu.CompilerParams(vmem_limit_bytes=VMEM_LIMIT, **extra),
    )(*ins)


def body(frames_in, sp_qkv, sp_out, tm_qkv, tm_out, cotangent):
    x = frames_in.reshape(T, D)
    cot = cotangent.reshape(T, D)
    shards = (sp_qkv, sp_out, tm_qkv, tm_out)
    dma = pltpu.SemaphoreType.DMA
    sp_qkv, sp_out, tm_qkv, tm_out = call(
        gather_kernel, shards, [sds((D, w.shape[1]), BF16) for w in shards],
        [dma((4 * GATHER_COPIES,)), dma((4 * GATHER_COPIES,)), dma((4,))],
        collective=0, specs=[ANY] * 4, out_specs=[ANY] * 4,
    )
    qkv, chunks = call(
        spatial_kernel, (x, sp_qkv, sp_out), [sds((T, 3 * D), BF16), sds((T, D), BF16)],
        [pltpu.VMEM((T, D), BF16), pltpu.VMEM((T, D), BF16)],
    )

    def exchange(rows):
        return lax.all_to_all(
            rows.reshape(32, 16, D), "frame", split_axis=0, concat_axis=0, tiled=True
        ).reshape(T, D)

    block_out, d_chunks, low, d_qkv = call(
        temporal_kernel, (exchange(chunks), cot, tm_qkv, tm_out),
        [sds((T, D), BF16), sds((T, D), BF16), sds((T, D), BF16), sds((T, 3 * D), BF16)],
        [
            pltpu.VMEM((T, D), BF16), pltpu.VMEM((T, 3 * D), BF16), pltpu.VMEM((T, D), BF16),
            pltpu.VMEM((T, D), BF16), pltpu.VMEM((CLIP, CLIP), F32), pltpu.VMEM((T, D), F32),
        ],
    )
    (grad_tm,) = call(
        reduce_kernel, (low, d_qkv), [sds((256, 3 * D), F32)],
        [
            pltpu.VMEM((2, 256, 3 * D), BF16), pltpu.VMEM((2, 256, 3 * D), BF16),
            pltpu.VMEM((2, 256, 3 * D), BF16),
            pltpu.VMEM((2, 64, 3 * D), BF16), pltpu.VMEM((2, 2, 64, 3 * D), BF16),
            pltpu.VMEM((2, 16, 3 * D), BF16), pltpu.VMEM((2, 2, 16, 3 * D), BF16),
            pltpu.VMEM((16, 3 * D), BF16), pltpu.VMEM((2, 16, 3 * D), BF16),
            pltpu.VMEM((256, 3 * D), BF16),
            dma((REDUCE_COPIES,)), dma((REDUCE_COPIES,)),
        ],
        collective=1,
    )
    (grad_in,) = call(
        spatial_back_kernel, (x, exchange(d_chunks), qkv, sp_qkv, sp_out), [sds((T, D), F32)],
        [pltpu.VMEM((T, D), BF16), pltpu.VMEM((T, D), BF16), pltpu.VMEM((T, 3 * D), BF16)],
    )
    return (block_out.reshape(cotangent.shape), grad_in.reshape(frames_in.shape), grad_tm)


def solution(mesh):
    in_specs = (
        P("fsdp", "frame", None, None),
        P("fsdp", None),
        P("fsdp", None),
        P("fsdp", None),
        P("fsdp", None),
        P("fsdp", None, "frame", None),
    )
    out_specs = (P("fsdp", None, "frame", None), P("fsdp", "frame", None, None), P("fsdp", None))
    return jax.shard_map(body, mesh=mesh, in_specs=in_specs, out_specs=out_specs, check_vma=False)
```

time: 2120 us -> 313 us (0.15)
  waiting for transfers between devices: 1910 us -> 0.01 us
  Pallas kernels: 0 us -> 280 us
  matrix products: 107 us -> 0 us
  local copies, waits for them, and re-layouts: 46.6 us -> 2.63 us
  blocking collectives: 0 us -> 23.9 us
    all_gather x5 -> x0, waiting for transfers between devices: 1290 us -> none  [the longest x4 1180 us: gather_rows(): return lax.all_gather(mine, ('fsdp', 'frame'), axis=0, tiled=True)]
    reduce_scatter x1 -> x0, waiting for transfers between devices: 612 us -> none  [body(): lax.psum_scatter(lax.dot_general(left_rows, right_rows, (((0,), (0,)), ((...]
    pallas_call x0 -> x5, Pallas kernels: none -> 280 us  [call(): pl.pallas_call(kernel, out_shape=outs, in_specs=specs or [VM] * len(ins),...]
    dot_general x19 -> x0, matrix products: 96.2 us -> none  [the longest x4 21.1 us: times(): prod = jnp.dot(flat, weight, preferred_element_type=jnp.float32)]
    all_to_all x0 -> x1, blocking collectives: none -> 23.9 us  [exchange(): lax.all_to_all(rows.reshape(32, 16, D), 'frame', split_axis=0, concat_axi...]
  transfers between devices with their start and end apart: 8 -> 1, of which waited for: 7 -> 0; matrix products, arithmetic and copies ran while one was open for 5% -> 0% of each run, Pallas kernels for 0% -> 22%
where the time goes in v2:
time: 313 us; the launch traced here: 312 us
  Pallas kernels  280 us (89%)
  blocking collectives  23.9 us (8%)
  starting transfers between devices  4.53 us (1%)
    pallas_call x5, Pallas kernels, call(): pl.pallas_call(kernel, out_shape=outs, in_specs=specs or [VM] * len(ins),...  280 us
    all_to_all x1, blocking collectives, exchange(): lax.all_to_all(rows.reshape(32, 16, D), 'frame', split_axis=0, concat_axi...  23.9 us
  transfers between devices with their start and end apart: 1, of which 0 were waited for; matrix products, arithmetic and copies ran while one was open for 0% of the time, Pallas kernels for 22%

profile of v2, /device:TPU:0, one launch (start us, length us, event | category | flops | bytes accessed | tf_op | source)
XLA Modules:
  0.0 312.0 jit_solution(16300600539305621493)
XLA Ops:
  0.6 133.4 %shard_map.85 = (bf16[1024,3072]{1,0:T(8,128)(2,1)}, bf16[1024,1024]{1,0:T(8,128)(2,1)}, bf16[1024,3072]{1,0:T(8,128)(2,1)}, bf16[1024,1024]{1,0:T(8,128)(2,1)}) custom-call(bf16[256,3072]{1,0:T(8,128)(2,1)} %refs_0_.1, bf16[256,1024]{1,0:T(8,128)(2,1)} %refs_1_.1, bf16[256,3072]{1,0:T(8,128)(2,1)} %refs_2_.1, bf16[256,1024]{1,0:T(8,128)(2,1)} %refs_3_.1), custom_call_target="tpu_custom_call" | custom-call | tf_op jit(solution)/shard_map/pallas_call | solution.py:457
  134.1 20.4 %shard_map.86 = (bf16[512,3072]{1,0:T(8,128)(2,1)}, bf16[512,1024]{1,0:T(8,128)(2,1)}) custom-call(bf16[512,1024]{1,0:T(8,128)(2,1)} %bitcast.11, bf16[1024,3072]{1,0:T(8,128)(2,1)} %get-tuple-element.13.wqkv_ref, bf16[1024,1024]{1,0:T(8,128)(2,1)} %get-tuple-element.14.wo_ref), custom_call_target="tpu_custom_call" | custom-call | tf_op jit(solution)/shard_map/pallas_call | solution.py:457
  154.5 23.9 %all_to_all.10 = bf16[32,16,1024]{2,1,0:T(8,128)(2,1)} all-to-all(bf16[32,16,1024]{2,1,0:T(8,128)(2,1)} %bitcast.17), channel_id=1, replica_groups=mesh['frame'=32,'fsdp'=4] {'frame'}, dimensions={0} | all-to-all | bytes 2097152 | tf_op jit(solution)/shard_map/all_to_all | solution.py:483
  178.4 34.2 %shard_map.87 = (bf16[512,1024]{1,0:T(8,128)(2,1)}, bf16[512,1024]{1,0:T(8,128)(2,1)}, bf16[512,1024]{1,0:T(8,128)(2,1)}, bf16[512,3072]{1,0:T(8,128)(2,1)}) custom-call(bf16[512,1024]{1,0:T(8,128)(2,1)} %bitcast.10, bf16[512,1024]{1,0:T(8,128)(2,1)} %bitcast.15, bf16[1024,3072]{1,0:T(8,128)(2,1)} %get-tuple-element.16.wqkv_ref, ...), custom_call_target="tpu_custom_call" | custom-call | tf_op jit(solution)/shard_map/pallas_call | solution.py:457
  212.6 4.5 %all-to-all-start.1 = ((bf16[32,16,1024]{2,1,0:T(8,128)(2,1)}), bf16[32,16,1024]{2,1,0:T(8,128)(2,1)S(1)}, u32[]{:S(2)}, u32[]{:S(2)}) async-start(bf16[32,16,1024]{2,1,0:T(8,128)(2,1)} %bitcast.16), calls=%async_computation.1 | async-start | bytes 2097152 | tf_op jit(solution)/shard_map/all_to_all | solution.py:483
  217.2 67.4 %shard_map.89 = f32[256,3072]{1,0:T(8,128)} custom-call(bf16[512,1024]{1,0:T(8,128)(2,1)} %get-tuple-element.21.low_ref, bf16[512,3072]{1,0:T(8,128)(2,1)} %get-tuple-element.22.dq_ref), custom_call_target="tpu_custom_call" | custom-call | tf_op jit(solution)/shard_map/pallas_call | solution.py:457
  284.6 0.0 all-to-all-done.1
  284.6 0.0 copy-start.1
  284.6 1.0 copy-done.1
  285.6 0.0 copy-start
  285.6 24.8 %shard_map.88 = f32[512,1024]{1,0:T(8,128)} custom-call(bf16[512,1024]{1,0:T(8,128)(2,1)} %bitcast.12, bf16[512,1024]{1,0:T(8,128)(2,1)} %bitcast.13, bf16[512,3072]{1,0:T(8,128)(2,1)} %get-tuple-element.20.qkv_ref, bf16[1024,3072]{1,0:T(8,128)(2,1)} %get-tuple-element.13.wqkv_ref, bf16[1024,1024]{1,0:T(8,128)(2,1)} %get-tuple-element.14.wo_ref), custom_call_target="tpu_custom_call" | custom-call | tf_op jit(solution)/shard_map/pallas_call | solution.py:457
  310.4 0.0 copy-done
  310.4 1.7 copy.11
Async XLA Ops:
  212.6 71.9 %all-to-all-start.1 = ((bf16[32,16,1024]{2,1,0:T(8,128)(2,1)}), bf16[32,16,1024]{2,1,0:T(8,128)(2,1)S(1)}, u32[]{:S(2)}, u32[]{:S(2)}) async-start(bf16[32,16,1024]{2,1,0:T(8,128)(2,1)} %bitcast.16), calls=%async_computation.1 | async-start | bytes 2097152 | tf_op jit(solution)/shard_map/all_to_all | solution.py:483
  284.6 1.0 copy-start.1
  285.6 24.8 %copy-start = (f32[256,3072]{1,0:T(8,128)S(1)}, f32[256,3072]{1,0:T(8,128)}, u32[]{:S(2)}) copy-start(f32[256,3072]{1,0:T(8,128)} %shard_map.89) | copy-start | bytes 9437188

commit v3 on v1

v3 whole, which is shorter than its diff:
```python
import functools

import jax
import jax.numpy as jnp
from jax import lax
from jax.experimental import pallas as pl
from jax.experimental.pallas import tpu as pltpu
from jax.sharding import PartitionSpec as P

MESH = pl.DeviceIdType.MESH
F32 = jnp.float32
BF16 = jnp.bfloat16
EPS = 1e-05
HEADS = 8
HEAD = 128
SCALE = HEAD**-0.5
D = 1024
T = 512
CLIP = 256
VMEM_LIMIT = 60 * 1024 * 1024


def dot(left, right):
    return lax.dot_general(left, right, (((1,), (0,)), ((), ())), preferred_element_type=F32)


def dot_nt(left, right):
    return lax.dot_general(left, right, (((1,), (1,)), ((), ())), preferred_element_type=F32)


def dot_tn(left, right):
    return lax.dot_general(left, right, (((0,), (0,)), ((), ())), preferred_element_type=F32)


def ds(index, size):
    return pl.ds(pl.multiple_of(index * size, size), size)


def loop(count, unroll=1):
    def run(body):
        def step(i, carry):
            body(i)
            return carry

        lax.fori_loop(0, count, step, 0, unroll=unroll)

    return run


def normalize(u):
    mean = jnp.mean(u, axis=-1, keepdims=True)
    cent = u - mean
    rstd = lax.rsqrt(jnp.mean(cent * cent, axis=-1, keepdims=True) + EPS)
    return cent * rstd, rstd


def norm_back(normed, rstd, grad):
    first = jnp.mean(grad, axis=-1, keepdims=True)
    second = jnp.mean(grad * normed, axis=-1, keepdims=True)
    return rstd * (grad - first - normed * second)


def softmax(scores):
    top = jnp.max(scores, axis=-1, keepdims=True)
    expo = jnp.exp(scores - top)
    return expo / jnp.sum(expo, axis=-1, keepdims=True)


def attend_back(q, k, v, probs, low, a):
    d_probs = dot_nt(a, v)
    d_v = dot_tn(low, a)
    prod = d_probs * probs
    d_s = ((prod - probs * jnp.sum(prod, axis=-1, keepdims=True)) * SCALE).astype(BF16)
    return dot(d_s, k), dot_tn(d_s, q), d_v


def part(i, head):
    return pl.ds(pl.multiple_of((i * HEADS + head) * HEAD, HEAD), HEAD)


def rows_at(index, size):
    return pl.ds(pl.multiple_of(index, size), size)


class Place:
    def __init__(self):
        frame, fsdp = lax.axis_index("frame"), lax.axis_index("fsdp")
        self.lo, x, y = lax.div(frame, 16), lax.rem(lax.div(frame, 4), 4), lax.rem(frame, 4)
        self.hi, self.core = lax.div(fsdp, 2), lax.rem(fsdp, 2)
        self.x, self.y = x, y
        self.a = x + self.core * (y - x)
        self.b = y + self.core * (x - y)
        self.ap, self.am = lax.rem(self.a + 1, 4), lax.rem(self.a + 3, 4)
        self.bp, self.bm = lax.rem(self.b + 1, 4), lax.rem(self.b + 3, 4)
        self.a2, self.b2 = lax.rem(self.a + 2, 4), lax.rem(self.b + 2, 4)
        self.fsdp, self.frame = fsdp, frame
        self.far = (frame, (1 - self.hi) * 2 + self.core)
        self.sibling = (frame, self.hi * 2 + 1 - self.core)
        self.cross = ((1 - self.lo) * 16 + x * 4 + y, (1 - self.hi) * 2 + self.core)
        self.twin = ((1 - self.lo) * 16 + x * 4 + y, fsdp)
        self.a_next, self.a_prev = self.at(self.ap, self.b), self.at(self.am, self.b)
        self.b_next, self.b_prev = self.at(self.a, self.bp), self.at(self.a, self.bm)

    def at(self, a, b):
        x = a + self.core * (b - a)
        y = b + self.core * (a - b)
        return (self.lo * 16 + x * 4 + y, self.fsdp)


class Copies:
    def __init__(self, send, recv):
        self.send, self.recv, self.count, self.started = send, recv, 0, []

    def start(self, src, dst, device):
        i = self.count
        self.count += 1
        copy = pltpu.make_async_remote_copy(
            src_ref=src, dst_ref=dst, send_sem=self.send.at[i], recv_sem=self.recv.at[i],
            device_id=device, device_id_type=MESH,
        )
        copy.start()
        self.started.append(copy)
        return copy

    def finish(self):
        for copy in self.started:
            copy.wait_send()


def rows_at(index, size):
    return pl.ds(pl.multiple_of(index, size), size)


def exchange_start(here, send, recv, clip, sems):
    recv[clip, here.frame] = send[clip, here.frame]

    @loop(31)
    def _(d):
        peer = lax.rem(here.frame + 1 + d, 32)
        pltpu.make_async_remote_copy(
            src_ref=send.at[clip, peer], dst_ref=recv.at[clip, here.frame],
            send_sem=sems.at[0, clip], recv_sem=sems.at[1, clip],
            device_id=(peer, here.fsdp), device_id_type=MESH,
        ).start()


def exchange_wait(buffer, clip, sem):
    block = buffer.at[clip, pl.ds(0, 31)]
    pltpu.make_async_copy(block, block, sem).wait()


def gather(copies, here, shard, out):
    own = here.fsdp * 256
    base = ((1 - here.hi) * 2 + here.core) * 256
    piece = (here.b * 4 + here.a) * 16
    cross = copies.start(
        shard.at[rows_at(piece, 16), :], out.at[rows_at(own + piece, 16), :], here.cross
    )
    mine = copies.start(shard, out.at[rows_at(own, 256), :], here.sibling)
    yield
    cross.wait_recv()
    block = out.at[rows_at(base + piece, 16), :]
    sent = [copies.start(block, block, here.at(a, here.b)) for a in (here.ap, here.am, here.a2)]
    yield
    for copy in sent:
        copy.wait_recv()
    block = out.at[rows_at(base + here.b * 64, 64), :]
    sent = [copies.start(block, block, here.at(here.a, b)) for b in (here.bp, here.bm, here.b2)]
    over = [copies.start(block, block, here.sibling)]
    yield
    for copy in sent:
        copy.wait_recv()
    for b in (here.bp, here.bm, here.b2):
        block = out.at[rows_at(base + b * 64, 64), :]
        over.append(copies.start(block, block, here.sibling))
    yield
    mine.wait_recv()
    for copy in over:
        copy.wait_recv()


def reduce_chunk(copies, here, s, g, out):
    give, take, held, rb, ra, rz, total = (
        r.at[g] for r in (s.give, s.take, s.held, s.rb, s.ra, s.rz, s.total)
    )
    for h in range(2):
        for i in range(3):
            cols = pl.ds(i * D + g * 256, 256)
            to = pl.ds(i * 256, 256)
            for core, ref in ((1 - here.core, give), (here.core, held)):
                left = s.low_t[rows_at((h * 2 + core) * 256, 256), :]
                ref[h, :, to] = dot(left, s.dqkv[:, cols]).astype(BF16)
    over = copies.start(give, take, here.sibling)
    yield
    over.wait_recv()
    for h in range(2):
        held[h] = (held[h].astype(F32) + take[h].astype(F32)).astype(BF16)

    def scatter(size, offset, at, others, device, dst):
        sent = []
        for i, other in enumerate(others):
            block = held.at[:, rows_at(offset + other * size, size), :]
            sent.append(copies.start(block, dst.at[i], device(other)))
        yield
        for copy in sent:
            copy.wait_recv()
        rows = rows_at(offset + at * size, size)
        sum_ = held[:, rows, :].astype(F32)
        for i in range(3):
            sum_ = sum_ + dst[i].astype(F32)
        held[:, rows, :] = sum_.astype(BF16)

    base = here.b * 64
    yield from scatter(
        64, 0, here.b, (here.bp, here.b2, here.bm), lambda b: here.at(here.a, b), rb
    )
    yield from scatter(
        16, base, here.a, (here.ap, here.a2, here.am), lambda a: here.at(a, here.b), ra
    )

    mine = rows_at(base + here.a * 16, 16)
    slot = here.lo * 2 + here.hi
    rz[slot] = held[here.hi, mine, :]
    sent = [
        copies.start(held.at[1 - here.hi, mine, :], rz.at[slot], here.cross),
        copies.start(held.at[1 - here.hi, mine, :], rz.at[slot], here.far),
        copies.start(held.at[here.hi, mine, :], rz.at[slot], here.twin),
    ]
    yield
    for copy in sent:
        copy.wait_recv()
    sum_ = rz[0].astype(F32)
    for i in range(1, 4):
        sum_ = sum_ + rz[i].astype(F32)
    total[mine, :] = sum_.astype(BF16)

    block = total.at[mine, :]
    sent = [copies.start(block, block, here.at(a, here.b)) for a in (here.ap, here.am, here.a2)]
    yield
    for copy in sent:
        copy.wait_recv()
    block = total.at[rows_at(base, 64), :]
    sent = [copies.start(block, block, here.at(here.a, b)) for b in (here.bp, here.bm, here.b2)]
    yield
    for copy in sent:
        copy.wait_recv()
    for i in range(3):
        out[:, pl.ds(i * D + g * 256, 256)] = total[:, pl.ds(i * 256, 256)].astype(F32)


def kernel(names, *refs):
    s = Scratch(zip(names, refs))
    here = Place()
    loads = {}
    for i, (src, dst) in enumerate((
        (s.x_hbm, s.x),
        (s.sp_qkv, s.wsq.at[rows_at(here.fsdp * 256, 256), :]),
        (s.sp_out, s.wso.at[rows_at(here.fsdp * 256, 256), :]),
        (s.tm_qkv, s.wtq.at[rows_at(here.fsdp * 256, 256), :]),
        (s.tm_out, s.wto.at[rows_at(here.fsdp * 256, 256), :]),
        (s.cot_hbm, s.cot),
    )):
        loads[i] = pltpu.make_async_copy(src, dst, s.local.at[i])
        loads[i].start()

    barrier = pltpu.get_barrier_semaphore()

    @loop(31)
    def _(d):
        peer = lax.rem(here.frame + 1 + d, 32)
        pl.semaphore_signal(barrier, inc=1, device_id=(peer, here.fsdp), device_id_type=MESH)

    for device in (here.sibling, here.cross, here.far):
        pl.semaphore_signal(barrier, inc=1, device_id=device, device_id_type=MESH)
    pl.semaphore_wait(barrier, 34)

    copies = Copies(s.send, s.recv)
    thirds = [pl.ds(i * D, D) for i in range(3)]
    sp = [gather(copies, here, s.sp_qkv.at[:, c], s.wsq.at[:, c]) for c in thirds]
    sp.append(gather(copies, here, s.sp_out, s.wso))
    tm = [gather(copies, here, s.tm_qkv, s.wtq), gather(copies, here, s.tm_out, s.wto)]

    def pump(active, times=1):
        for _ in range(times):
            for steps in active:
                next(steps, None)

    def drain(steps):
        for _ in steps:
            pass

    pump(sp)
    loads[0].wait()

    @loop(8)
    def _(r):
        rows = ds(r, 64)
        s.nrm[rows, :] = normalize(s.x[rows, :].astype(F32))[0].astype(BF16)

    row = lax.broadcasted_iota(jnp.int32, (CLIP, CLIP), 0)
    col = lax.broadcasted_iota(jnp.int32, (CLIP, CLIP), 1)
    allowed = (col <= row) & (((row - col) & 7) == 0)
    s.bias[...] = jnp.where(allowed, 0.0, -1e30)

    pump(sp, 3)
    loads[1].wait()
    for i in range(3):
        drain(sp[i])
        if i == 1:
            pump(tm)

        @loop(2)
        def _(n):
            cols = pl.ds(pl.multiple_of(i * D + n * 512, 512), 512)
            s.qkv[:, cols] = dot(s.nrm[...], s.wsq[:, cols]).astype(BF16)

    pump(tm)
    drain(sp[3])
    loads[2].wait()
    for c in range(2):
        rows = pl.ds(c * CLIP, CLIP)

        @loop(4)
        def _(n):
            for j in range(2):
                q, k, v = (s.qkv[rows, part(i, 2 * n + j)] for i in range(3))
                low = softmax(dot_nt(q, k) * SCALE).astype(BF16)
                s.att[rows, part(0, 2 * n + j)] = dot(low, v).astype(BF16)

        pump(tm)

        @loop(4)
        def _(n):
            cols = ds(n, 256)
            out = dot(s.att[rows, :], s.wso[:, cols]) + s.x[rows, cols].astype(F32)
            s.send_s[c, :, :, cols] = out.reshape(32, 8, 256).astype(BF16)

        exchange_start(here, s.send_s, s.recv_s, c, s.sem_s)

    for steps in tm[::-1]:
        drain(steps)
    for i in (3, 4, 5):
        loads[i].wait()

    @loop(2)
    def _(n):
        cols = ds(n, 512)
        s.da[:, cols] = dot_nt(s.cot[...], s.wto[cols, :]).astype(BF16)

    for c in range(2):
        exchange_wait(s.recv_s, c, s.sem_s.at[1, c])

        @loop(4)
        def _(r):
            rows = rows_at(c * CLIP + r * 64, 64)
            u = s.recv_s[c, ds(r, 8)].astype(F32).reshape(64, D)
            s.low[rows, :] = normalize(u)[0].astype(BF16)

        rows = pl.ds(c * CLIP, CLIP)
        s.low_t[:, rows] = s.low[rows, :].T

        @loop(6)
        def _(n):
            cols = ds(n, 512)
            s.tqkv[rows, cols] = dot(s.low[rows, :], s.wtq[:, cols]).astype(BF16)

    reducing = []
    for g in range(4):

        @loop(2)
        def _(n):
            h = g * 2 + n
            for c in range(2):
                rows = pl.ds(c * CLIP, CLIP)
                q, k, v = (s.tqkv[rows, part(i, h)] for i in range(3))
                probs = softmax(dot_nt(q, k) * SCALE + s.bias[...])
                low = probs.astype(BF16)
                s.att[rows, part(0, h)] = dot(low, v).astype(BF16)
                parts = attend_back(q, k, v, probs, low, s.da[rows, part(0, h)])
                for i in range(3):
                    s.dqkv[rows, part(i, h)] = parts[i].astype(BF16)

        pump(reducing)
        reducing.append(reduce_chunk(copies, here, s, g, s.gtm))
        pump(reducing[-1:])

    for c in range(2):
        rows = pl.ds(c * CLIP, CLIP)

        @loop(4)
        def _(n):
            cols = ds(n, 256)
            s.gin[rows, cols] = dot_nt(s.dqkv[rows, :], s.wtq[cols, :])

        @loop(4)
        def _(r):
            rows = rows_at(c * CLIP + r * 64, 64)
            normed, rstd = normalize(s.recv_s[c, ds(r, 8)].astype(F32).reshape(64, D))
            grad = s.cot[rows, :].astype(F32) + norm_back(normed, rstd, s.gin[rows, :])
            s.send_d[c, ds(r, 8)] = grad.reshape(8, 8, D).astype(BF16)

        exchange_start(here, s.send_d, s.recv_d, c, s.sem_d)
        pump(reducing)

    for c in range(2):

        @loop(2)
        def _(n):
            cols = ds(n, 512)
            rows = pl.ds(c * CLIP, CLIP)
            stream = s.recv_s[c, :, :, cols].astype(F32).reshape(CLIP, 512)
            s.block_out[rows, cols] = (dot(s.att[rows, :], s.wto[:, cols]) + stream).astype(BF16)

    pump(reducing)
    for c in range(2):
        rows = pl.ds(c * CLIP, CLIP)
        exchange_wait(s.recv_d, c, s.sem_d.at[1, c])

        @loop(4)
        def _(r):
            rows = rows_at(c * CLIP + r * 64, 64)
            s.low[rows, :] = s.recv_d[c, ds(r, 8)].astype(F32).reshape(64, D).astype(BF16)

        @loop(2)
        def _(n):
            cols = ds(n, 512)
            s.da[rows, cols] = dot_nt(s.low[rows, :], s.wso[cols, :]).astype(BF16)

        for g in range(2):

            @loop(4)
            def _(n):
                h = g * 4 + n
                q, k, v = (s.qkv[rows, part(i, h)] for i in range(3))
                probs = softmax(dot_nt(q, k) * SCALE)
                parts = attend_back(q, k, v, probs, probs.astype(BF16), s.da[rows, part(0, h)])
                for i in range(3):
                    s.tqkv[rows, part(i, h)] = parts[i].astype(BF16)

            pump(reducing)

        @loop(4)
        def _(n):
            cols = ds(n, 256)
            s.gin[rows, cols] = dot_nt(s.tqkv[rows, :], s.wsq[cols, :])

        pump(reducing)

        @loop(4)
        def _(r):
            rows = rows_at(c * CLIP + r * 64, 64)
            normed, rstd = normalize(s.x[rows, :].astype(F32))
            s.gin[rows, :] = s.low[rows, :].astype(F32) + norm_back(normed, rstd, s.gin[rows, :])

    while reducing:
        pump(reducing)
        reducing = [r for r in reducing if r.gi_frame is not None]
    copies.finish()
    for c in range(2):
        exchange_wait(s.send_s, c, s.sem_s.at[0, c])
        exchange_wait(s.send_d, c, s.sem_d.at[0, c])


class Scratch:
    def __init__(self, pairs):
        for name, ref in pairs:
            setattr(self, name, ref)


VM = pl.BlockSpec(memory_space=pltpu.VMEM)
ANY = pl.BlockSpec(memory_space=pl.ANY)


def body(frames_in, sp_qkv, sp_out, tm_qkv, tm_out, cotangent):
    low = lambda *shape: pltpu.VMEM(shape, BF16)
    dma = pltpu.SemaphoreType.DMA
    scratch = dict(
        x=low(T, D), cot=low(T, D), wsq=low(D, 3 * D), wso=low(D, D), wtq=low(D, 3 * D), wto=low(D, D),
        nrm=low(T, D), qkv=low(T, 3 * D), att=low(T, D), low=low(T, D), low_t=low(D, T),
        tqkv=low(T, 3 * D), da=low(T, D), dqkv=low(T, 3 * D), bias=pltpu.VMEM((CLIP, CLIP), F32),
        send_s=low(2, 32, 8, D), recv_s=low(2, 32, 8, D),
        send_d=low(2, 32, 8, D), recv_d=low(2, 32, 8, D),
        give=low(4, 2, 256, 768), take=low(4, 2, 256, 768), held=low(4, 2, 256, 768),
        rb=low(4, 3, 2, 64, 768), ra=low(4, 3, 2, 16, 768), rz=low(4, 4, 16, 768),
        total=low(4, 256, 768),
        local=dma((6,)), send=dma((COPIES,)), recv=dma((COPIES,)), sem_s=dma((2, 2)), sem_d=dma((2, 2)),
    )
    names = ["x_hbm", "sp_qkv", "sp_out", "tm_qkv", "tm_out", "cot_hbm", "block_out", "gin", "gtm"]
    block_out, grad_in, grad_tm = pl.pallas_call(
        functools.partial(kernel, names + list(scratch)),
        out_shape=[
            jax.ShapeDtypeStruct((T, D), BF16),
            jax.ShapeDtypeStruct((T, D), F32),
            jax.ShapeDtypeStruct((256, 3 * D), F32),
        ],
        in_specs=[ANY] * 6,
        out_specs=[VM] * 3,
        scratch_shapes=list(scratch.values()),
        compiler_params=pltpu.CompilerParams(
            vmem_limit_bytes=VMEM_LIMIT, collective_id=0, has_side_effects=True
        ),
        name="block",
    )(frames_in.reshape(T, D), sp_qkv, sp_out, tm_qkv, tm_out, cotangent.reshape(T, D))
    return (block_out.reshape(cotangent.shape), grad_in.reshape(frames_in.shape), grad_tm)


COPIES = 6 * 12 + 4 * 16


def solution(mesh):
    in_specs = (
        P("fsdp", "frame", None, None),
        P("fsdp", None),
        P("fsdp", None),
        P("fsdp", None),
        P("fsdp", None),
        P("fsdp", None, "frame", None),
    )
    out_specs = (P("fsdp", None, "frame", None), P("fsdp", "frame", None, None), P("fsdp", None))
    return jax.shard_map(body, mesh=mesh, in_specs=in_specs, out_specs=out_specs, check_vma=False)
```

time: 2120 us -> 170 us (0.08)
  waiting for transfers between devices: 1910 us -> 0 us
  Pallas kernels: 0 us -> 163 us
  matrix products: 107 us -> 0 us
  local copies, waits for them, and re-layouts: 46.6 us -> 6.72 us
    all_gather x5 -> x0, waiting for transfers between devices: 1290 us -> none  [the longest x4 1180 us: gather_rows(): return lax.all_gather(mine, ('fsdp', 'frame'), axis=0, tiled=True)]
    reduce_scatter x1 -> x0, waiting for transfers between devices: 612 us -> none  [body(): lax.psum_scatter(lax.dot_general(left_rows, right_rows, (((0,), (0,)), ((...]
    pallas_call x0 -> x1, Pallas kernels: none -> 163 us  [body(): pl.pallas_call(functools.partial(kernel, names + list(scratch)), out_shap...]
    dot_general x19 -> x0, matrix products: 96.2 us -> none  [the longest x4 21.1 us: times(): prod = jnp.dot(flat, weight, preferred_element_type=jnp.float32)]
  transfers between devices with their start and end apart: 8 -> 0, of which waited for: 7 -> 0; matrix products, arithmetic and copies ran while one was open for 5% -> 0% of each run, Pallas kernels for 0% -> 0%
where the time goes in v3:
time: 170 us
  Pallas kernels  163 us (96%)
  local copies, waits for them, and re-layouts  6.72 us (4%)
    pallas_call x1, Pallas kernels, body(): pl.pallas_call(functools.partial(kernel, names + list(scratch)), out_shap...  163 us
    unnamed x7, local copies, waits for them, and re-layouts  6.72 us

profile of v3, /device:TPU:0, one launch (start us, length us, event | category | flops | bytes accessed | tf_op | source)
XLA Modules:
  0.0 170.2 jit_solution(7250207146925742657)
XLA Ops:
  0.6 162.9 %block.1 = (bf16[512,1024]{1,0:T(8,128)(2,1)}, f32[512,1024]{1,0:T(8,128)}, f32[256,3072]{1,0:T(8,128)}) custom-call(bf16[512,1024]{1,0:T(8,128)(2,1)} %bitcast.8, bf16[256,3072]{1,0:T(8,128)(2,1)} %refs_1_.1, bf16[256,1024]{1,0:T(8,128)(2,1)} %refs_2_.1, bf16[256,3072]{1,0:T(8,128)(2,1)} %refs_3_.1, bf16[256,1024]{1,0:T(8,128)(2,1)} %refs_4_.1, ...), custom_call_target="tpu_custom_call" | custom-call | tf_op jit(solution)/shard_map/block/pallas_call | solution.py:489
  163.5 0.0 copy-start.1
  163.5 2.4 %copy.13 = bf16[2,32,8,1024]{3,2,1,0:T(8,128)(2,1)} copy(bf16[2,32,8,1024]{3,2,1,0:T(8,128)(2,1)} %bitcast.7) | data formatting | bytes 2097152
  165.9 0.0 copy-done.1
  165.9 0.0 copy-start
  165.9 1.3 copy.14
  167.2 1.3 copy-done
  168.6 1.7 copy.15
Async XLA Ops:
  163.5 2.4 %copy-start.1 = (f32[512,1024]{1,0:T(8,128)S(1)}, f32[512,1024]{1,0:T(8,128)}, u32[]{:S(2)}) copy-start(f32[512,1024]{1,0:T(8,128)} %get-tuple-element.7) | copy-start | bytes 6291460
  165.9 2.6 %copy-start = (f32[256,3072]{1,0:T(8,128)S(1)}, f32[256,3072]{1,0:T(8,128)}, u32[]{:S(2)}) copy-start(f32[256,3072]{1,0:T(8,128)} %get-tuple-element.17) | copy-start | bytes 9437188

commit v4 on v3

--- a/solution.py
+++ b/solution.py
@@ -66,16 +66,37 @@
     return expo / jnp.sum(expo, axis=-1, keepdims=True)
 
 
-def attend_back(q, k, v, probs, low, a):
-    d_probs = dot_nt(a, v)
-    d_v = dot_tn(low, a)
-    prod = d_probs * probs
-    d_s = ((prod - probs * jnp.sum(prod, axis=-1, keepdims=True)) * SCALE).astype(BF16)
-    return dot(d_s, k), dot_tn(d_s, q), d_v
-
-
 def part(i, head):
     return pl.ds(pl.multiple_of((i * HEADS + head) * HEAD, HEAD), HEAD)
+
+
+def attention(units, qkv, bias=None, att=None, d_att=None, d_qkv=None):
+    q, k, v = ([qkv[rows, part(i, head)] for rows, head in units] for i in range(3))
+    n = range(len(units))
+    scores = [dot_nt(q[i], k[i]) * SCALE for i in n]
+    if d_att is not None:
+        a = [d_att[rows, part(0, head)] for rows, head in units]
+        d_probs = [dot_nt(a[i], v[i]) for i in n]
+    if bias is not None:
+        scores = [scores[i] + bias[...] for i in n]
+    probs = [softmax(scores[i]) for i in n]
+    low = [probs[i].astype(BF16) for i in n]
+    if att is not None:
+        for i, (rows, head) in enumerate(units):
+            att[rows, part(0, head)] = dot(low[i], v[i]).astype(BF16)
+    if d_att is None:
+        return
+    for i, (rows, head) in enumerate(units):
+        d_qkv[rows, part(2, head)] = dot_tn(low[i], a[i]).astype(BF16)
+    prod = [d_probs[i] * probs[i] for i in n]
+    d_s = [
+        ((prod[i] - probs[i] * jnp.sum(prod[i], axis=-1, keepdims=True)) * SCALE).astype(BF16)
+        for i in n
+    ]
+    for i, (rows, head) in enumerate(units):
+        d_qkv[rows, part(0, head)] = dot(d_s[i], k[i]).astype(BF16)
+    for i, (rows, head) in enumerate(units):
+        d_qkv[rows, part(1, head)] = dot_tn(d_s[i], q[i]).astype(BF16)
 
 
 def rows_at(index, size):
@@ -101,6 +122,10 @@
         self.a_next, self.a_prev = self.at(self.ap, self.b), self.at(self.am, self.b)
         self.b_next, self.b_prev = self.at(self.a, self.bp), self.at(self.a, self.bm)
 
+    def across(self, a):
+        frame, _ = self.at(a, self.b)
+        return (frame + (1 - 2 * self.lo) * 16, (1 - self.hi) * 2 + self.core)
+
     def at(self, a, b):
         x = a + self.core * (b - a)
         y = b + self.core * (a - b)
@@ -127,10 +152,6 @@
             copy.wait_send()
 
 
-def rows_at(index, size):
-    return pl.ds(pl.multiple_of(index, size), size)
-
-
 def exchange_start(here, send, recv, clip, sems):
     recv[clip, here.frame] = send[clip, here.frame]
 
@@ -149,21 +170,24 @@
     pltpu.make_async_copy(block, block, sem).wait()
 
 
-def gather(copies, here, shard, out):
+def gather(copies, here, shard, out, wide):
     own = here.fsdp * 256
     base = ((1 - here.hi) * 2 + here.core) * 256
     piece = (here.b * 4 + here.a) * 16
-    cross = copies.start(
-        shard.at[rows_at(piece, 16), :], out.at[rows_at(own + piece, 16), :], here.cross
-    )
-    mine = copies.start(shard, out.at[rows_at(own, 256), :], here.sibling)
-    yield
-    cross.wait_recv()
-    block = out.at[rows_at(base + piece, 16), :]
-    sent = [copies.start(block, block, here.at(a, here.b)) for a in (here.ap, here.am, here.a2)]
+    row = (here.ap, here.am, here.a2)
+    src, dst = shard.at[rows_at(piece, 16), :], out.at[rows_at(own + piece, 16), :]
+    sent = [copies.start(src, dst, here.cross)]
+    if wide:
+        sent += [copies.start(src, dst, here.across(a)) for a in row]
     yield
     for copy in sent:
         copy.wait_recv()
+    if not wide:
+        block = out.at[rows_at(base + piece, 16), :]
+        sent = [copies.start(block, block, here.at(a, here.b)) for a in row]
+        yield
+        for copy in sent:
+            copy.wait_recv()
     block = out.at[rows_at(base + here.b * 64, 64), :]
     sent = [copies.start(block, block, here.at(here.a, b)) for b in (here.bp, here.bm, here.b2)]
     over = [copies.start(block, block, here.sibling)]
@@ -174,12 +198,29 @@
         block = out.at[rows_at(base + b * 64, 64), :]
         over.append(copies.start(block, block, here.sibling))
     yield
-    mine.wait_recv()
     for copy in over:
         copy.wait_recv()
 
 
-def reduce_chunk(copies, here, s, g, out):
+def gather_across(copies, here, shard, out):
+    half = rows_at(here.fsdp * 256 + (1 - here.lo) * 128, 128)
+    cross = copies.start(shard.at[rows_at((1 - here.lo) * 128, 128), :], out.at[half, :], here.cross)
+    yield
+    cross.wait_recv()
+    base = ((1 - here.hi) * 2 + here.core) * 256
+    block = out.at[rows_at(base + here.lo * 128, 128), :]
+    twin = copies.start(block, block, here.twin)
+    over = [copies.start(block, block, here.sibling)]
+    yield
+    twin.wait_recv()
+    block = out.at[rows_at(base + (1 - here.lo) * 128, 128), :]
+    over.append(copies.start(block, block, here.sibling))
+    yield
+    for copy in over:
+        copy.wait_recv()
+
+
+def reduce_chunk(copies, here, s, g, across_first):
     give, take, held, rb, ra, rz, total = (
         r.at[g] for r in (s.give, s.take, s.held, s.rb, s.ra, s.rz, s.total)
     )
@@ -195,20 +236,28 @@
     over.wait_recv()
     for h in range(2):
         held[h] = (held[h].astype(F32) + take[h].astype(F32)).astype(BF16)
+    shards, count = slice(None), 2
+    if across_first:
+        rx = s.rx.at[g]
+        cross = copies.start(held.at[1 - here.hi], rx, here.cross)
+        yield
+        cross.wait_recv()
+        held[here.hi] = (held[here.hi].astype(F32) + rx[...].astype(F32)).astype(BF16)
+        shards, count = pl.ds(here.hi, 1), 1
 
     def scatter(size, offset, at, others, device, dst):
         sent = []
         for i, other in enumerate(others):
-            block = held.at[:, rows_at(offset + other * size, size), :]
-            sent.append(copies.start(block, dst.at[i], device(other)))
+            block = held.at[shards, rows_at(offset + other * size, size), :]
+            sent.append(copies.start(block, dst.at[i, pl.ds(0, count)], device(other)))
         yield
         for copy in sent:
             copy.wait_recv()
         rows = rows_at(offset + at * size, size)
-        sum_ = held[:, rows, :].astype(F32)
+        sum_ = held[shards, rows, :].astype(F32)
         for i in range(3):
-            sum_ = sum_ + dst[i].astype(F32)
-        held[:, rows, :] = sum_.astype(BF16)
+            sum_ = sum_ + dst[i, :count].astype(F32)
+        held[shards, rows, :] = sum_.astype(BF16)
 
     base = here.b * 64
     yield from scatter(
@@ -219,19 +268,24 @@
     )
 
     mine = rows_at(base + here.a * 16, 16)
-    slot = here.lo * 2 + here.hi
-    rz[slot] = held[here.hi, mine, :]
-    sent = [
-        copies.start(held.at[1 - here.hi, mine, :], rz.at[slot], here.cross),
-        copies.start(held.at[1 - here.hi, mine, :], rz.at[slot], here.far),
-        copies.start(held.at[here.hi, mine, :], rz.at[slot], here.twin),
-    ]
+    own = held.at[here.hi, mine, :]
+    if across_first:
+        sent = [copies.start(own, rz.at[0], here.twin)]
+    else:
+        slot = here.lo * 2 + here.hi
+        rz[slot] = own[...]
+        other = held.at[1 - here.hi, mine, :]
+        sent = [copies.start(own, rz.at[slot], here.twin)]
+        sent += [copies.start(other, rz.at[slot], to) for to in (here.cross, here.far)]
     yield
     for copy in sent:
         copy.wait_recv()
     sum_ = rz[0].astype(F32)
-    for i in range(1, 4):
-        sum_ = sum_ + rz[i].astype(F32)
+    if across_first:
+        sum_ = sum_ + own[...].astype(F32)
+    else:
+        for i in range(1, 4):
+            sum_ = sum_ + rz[i].astype(F32)
     total[mine, :] = sum_.astype(BF16)
 
     block = total.at[mine, :]
@@ -245,7 +299,7 @@
     for copy in sent:
         copy.wait_recv()
     for i in range(3):
-        out[:, pl.ds(i * D + g * 256, 256)] = total[:, pl.ds(i * 256, 256)].astype(F32)
+        s.gtm[:, pl.ds(i * D + g * 256, 256)] = total[:, pl.ds(i * 256, 256)].astype(F32)
 
 
 def kernel(names, *refs):
@@ -270,75 +324,99 @@
         peer = lax.rem(here.frame + 1 + d, 32)
         pl.semaphore_signal(barrier, inc=1, device_id=(peer, here.fsdp), device_id_type=MESH)
 
-    for device in (here.sibling, here.cross, here.far):
+    near = [here.sibling, here.cross, here.far]
+    for device in near + [here.across(a) for a in (here.ap, here.am, here.a2)]:
         pl.semaphore_signal(barrier, inc=1, device_id=device, device_id_type=MESH)
-    pl.semaphore_wait(barrier, 34)
-
-    copies = Copies(s.send, s.recv)
+    copies = Copies(s.sent, s.got)
+
+    def drain(*many):
+        for steps in many:
+            for _ in steps:
+                pass
+
+    def step(*many):
+        for steps in many:
+            next(steps)
+
     thirds = [pl.ds(i * D, D) for i in range(3)]
-    sp = [gather(copies, here, s.sp_qkv.at[:, c], s.wsq.at[:, c]) for c in thirds]
-    sp.append(gather(copies, here, s.sp_out, s.wso))
-    tm = [gather(copies, here, s.tm_qkv, s.wtq), gather(copies, here, s.tm_out, s.wto)]
-
-    def pump(active, times=1):
-        for _ in range(times):
-            for steps in active:
-                next(steps, None)
-
-    def drain(steps):
-        for _ in steps:
-            pass
-
-    pump(sp)
+    halves = [[pl.ds(i * D + n * 512, 512) for i in range(3)] for n in range(2)]
+    sp = [
+        [gather(copies, here, s.sp_qkv.at[:, c], s.wsq.at[:, c], n == 0) for c in halves[n]]
+        for n in range(2)
+    ]
+    sp_out = gather_across(copies, here, s.sp_out, s.wso)
+    tm = [gather_across(copies, here, s.tm_qkv.at[:, c], s.wtq.at[:, c]) for c in thirds[:2]]
+    tm.append(gather(copies, here, s.tm_qkv.at[:, thirds[2]], s.wtq.at[:, thirds[2]], False))
+    tm_out = gather_across(copies, here, s.tm_out, s.wto)
+
     loads[0].wait()
 
     @loop(8)
     def _(r):
         rows = ds(r, 64)
-        s.nrm[rows, :] = normalize(s.x[rows, :].astype(F32))[0].astype(BF16)
+        s.low[rows, :] = normalize(s.x[rows, :].astype(F32))[0].astype(BF16)
+
+    pl.semaphore_wait(barrier, 37)
+    step(*sp[0], *sp[1])
+
+    def over(shard, out):
+        return copies.start(shard, out.at[rows_at(here.fsdp * 256, 256), :], here.sibling)
+
+    mine = [over(s.sp_qkv, s.wsq), over(s.sp_out, s.wso)]
+    step(sp_out, tm[2])
 
     row = lax.broadcasted_iota(jnp.int32, (CLIP, CLIP), 0)
     col = lax.broadcasted_iota(jnp.int32, (CLIP, CLIP), 1)
     allowed = (col <= row) & (((row - col) & 7) == 0)
     s.bias[...] = jnp.where(allowed, 0.0, -1e30)
 
-    pump(sp, 3)
+    step(*sp[0], *sp[1])
+    step(*sp[1])
+    step(sp_out)
+    step(tm[0], tm[1])
+    step(*sp[0])
+    mine[0].wait_recv()
     loads[1].wait()
-    for i in range(3):
-        drain(sp[i])
-        if i == 1:
-            pump(tm)
-
+
+    def project(n):
+        drain(*sp[n])
+        for i in range(3):
+            cols = halves[n][i]
+            s.qkv[:, cols] = dot(s.low[...], s.wsq[:, cols]).astype(BF16)
+
+    def attend(n):
         @loop(2)
-        def _(n):
-            cols = pl.ds(pl.multiple_of(i * D + n * 512, 512), 512)
-            s.qkv[:, cols] = dot(s.nrm[...], s.wsq[:, cols]).astype(BF16)
-
-    pump(tm)
-    drain(sp[3])
+        def _(c):
+            rows = rows_at(c * CLIP, CLIP)
+            attention([(rows, n * 4 + j) for j in range(4)], s.qkv, att=s.att)
+
+    project(0)
+    step(*sp[1])
+    step(tm[2])
+    attend(0)
+    project(1)
+    step(sp_out)
+    step(tm[2], tm[0], tm[1], tm_out)
+    mine += [over(s.tm_qkv, s.wtq), over(s.tm_out, s.wto)]
+    attend(1)
+    drain(sp_out)
+    mine[1].wait_recv()
     loads[2].wait()
     for c in range(2):
         rows = pl.ds(c * CLIP, CLIP)
 
         @loop(4)
         def _(n):
-            for j in range(2):
-                q, k, v = (s.qkv[rows, part(i, 2 * n + j)] for i in range(3))
-                low = softmax(dot_nt(q, k) * SCALE).astype(BF16)
-                s.att[rows, part(0, 2 * n + j)] = dot(low, v).astype(BF16)
-
-        pump(tm)
-
-        @loop(4)
-        def _(n):
             cols = ds(n, 256)
             out = dot(s.att[rows, :], s.wso[:, cols]) + s.x[rows, cols].astype(F32)
-            s.send_s[c, :, :, cols] = out.reshape(32, 8, 256).astype(BF16)
-
-        exchange_start(here, s.send_s, s.recv_s, c, s.sem_s)
-
-    for steps in tm[::-1]:
-        drain(steps)
+            s.send[c, :, :, cols] = out.reshape(32, 8, 256).astype(BF16)
+
+        exchange_start(here, s.send, s.recv_s, c, s.sem_s)
+
+    step(tm_out, tm[0], tm[1], tm[2], tm_out)
+    drain(*tm, tm_out)
+    mine[2].wait_recv()
+    mine[3].wait_recv()
     for i in (3, 4, 5):
         loads[i].wait()
 
@@ -359,30 +437,23 @@
         rows = pl.ds(c * CLIP, CLIP)
         s.low_t[:, rows] = s.low[rows, :].T
 
-        @loop(6)
-        def _(n):
-            cols = ds(n, 512)
-            s.tqkv[rows, cols] = dot(s.low[rows, :], s.wtq[:, cols]).astype(BF16)
-
-    reducing = []
+    def pump(*which):
+        for g in which:
+            next(chunks[g], None)
+
+    chunks = [reduce_chunk(copies, here, s, g, g < 2) for g in range(4)]
     for g in range(4):
 
-        @loop(2)
-        def _(n):
-            h = g * 2 + n
-            for c in range(2):
-                rows = pl.ds(c * CLIP, CLIP)
-                q, k, v = (s.tqkv[rows, part(i, h)] for i in range(3))
-                probs = softmax(dot_nt(q, k) * SCALE + s.bias[...])
-                low = probs.astype(BF16)
-                s.att[rows, part(0, h)] = dot(low, v).astype(BF16)
-                parts = attend_back(q, k, v, probs, low, s.da[rows, part(0, h)])
-                for i in range(3):
-                    s.dqkv[rows, part(i, h)] = parts[i].astype(BF16)
-
-        pump(reducing)
-        reducing.append(reduce_chunk(copies, here, s, g, s.gtm))
-        pump(reducing[-1:])
+        @loop(3)
+        def _(i):
+            cols = pl.ds(pl.multiple_of(i * D + g * 256, 256), 256)
+            s.tqkv[:, cols] = dot(s.low[...], s.wtq[:, cols]).astype(BF16)
+
+        units = [(pl.ds(c * CLIP, CLIP), g * 2 + n) for n in range(2) for c in range(2)]
+        attention(units, s.tqkv, s.bias, s.att, s.da, s.dqkv)
+        step(chunks[g])
+        if g > 0:
+            step(chunks[g - 1])
 
     for c in range(2):
         rows = pl.ds(c * CLIP, CLIP)
@@ -390,17 +461,19 @@
         @loop(4)
         def _(n):
             cols = ds(n, 256)
-            s.gin[rows, cols] = dot_nt(s.dqkv[rows, :], s.wtq[cols, :])
+            s.grad[rows, cols] = dot_nt(s.dqkv[rows, :], s.wtq[cols, :])
+
+        pump(*((3, 0), (2,))[c])
+        exchange_wait(s.send, c, s.sem_s.at[0, c])
 
         @loop(4)
         def _(r):
             rows = rows_at(c * CLIP + r * 64, 64)
             normed, rstd = normalize(s.recv_s[c, ds(r, 8)].astype(F32).reshape(64, D))
-            grad = s.cot[rows, :].astype(F32) + norm_back(normed, rstd, s.gin[rows, :])
-            s.send_d[c, ds(r, 8)] = grad.reshape(8, 8, D).astype(BF16)
-
-        exchange_start(here, s.send_d, s.recv_d, c, s.sem_d)
-        pump(reducing)
+            grad = s.cot[rows, :].astype(F32) + norm_back(normed, rstd, s.grad[rows, :])
+            s.send[c, ds(r, 8)] = grad.reshape(8, 8, D).astype(BF16)
+
+        exchange_start(here, s.send, s.recv_d, c, s.sem_d)
 
     for c in range(2):
 
@@ -411,7 +484,8 @@
             stream = s.recv_s[c, :, :, cols].astype(F32).reshape(CLIP, 512)
             s.block_out[rows, cols] = (dot(s.att[rows, :], s.wto[:, cols]) + stream).astype(BF16)
 
-    pump(reducing)
+        pump(*((0,), (2, 1))[c])
+
     for c in range(2):
         rows = pl.ds(c * CLIP, CLIP)
         exchange_wait(s.recv_d, c, s.sem_d.at[1, c])
@@ -426,39 +500,34 @@
             cols = ds(n, 512)
             s.da[rows, cols] = dot_nt(s.low[rows, :], s.wso[cols, :]).astype(BF16)
 
+        pump(*((3, 0), ())[c])
+
         for g in range(2):
 
-            @loop(4)
-            def _(n):
-                h = g * 4 + n
-                q, k, v = (s.qkv[rows, part(i, h)] for i in range(3))
-                probs = softmax(dot_nt(q, k) * SCALE)
-                parts = attend_back(q, k, v, probs, probs.astype(BF16), s.da[rows, part(0, h)])
-                for i in range(3):
-                    s.tqkv[rows, part(i, h)] = parts[i].astype(BF16)
-
-            pump(reducing)
+            units = [(rows, g * 4 + n) for n in range(4)]
+            attention(units, s.qkv, d_att=s.da, d_qkv=s.tqkv)
+            pump(*((2,), (1, 3, 0), (1, 3, 2), (0,))[c * 2 + g])
 
         @loop(4)
         def _(n):
             cols = ds(n, 256)
-            s.gin[rows, cols] = dot_nt(s.tqkv[rows, :], s.wsq[cols, :])
-
-        pump(reducing)
+            s.grad[rows, cols] = dot_nt(s.tqkv[rows, :], s.wsq[cols, :])
+
+        pump(*((2,), (1, 3))[c])
 
         @loop(4)
         def _(r):
             rows = rows_at(c * CLIP + r * 64, 64)
             normed, rstd = normalize(s.x[rows, :].astype(F32))
-            s.gin[rows, :] = s.low[rows, :].astype(F32) + norm_back(normed, rstd, s.gin[rows, :])
-
-    while reducing:
-        pump(reducing)
-        reducing = [r for r in reducing if r.gi_frame is not None]
+            grad = s.low[rows, :].astype(F32) + norm_back(normed, rstd, s.grad[rows, :])
+            s.gin[rows, :] = grad.astype(BF16)
+
+        pump(*((3, 1, 0), (1,))[c])
+
+    drain(*chunks)
     copies.finish()
     for c in range(2):
-        exchange_wait(s.send_s, c, s.sem_s.at[0, c])
-        exchange_wait(s.send_d, c, s.sem_d.at[0, c])
+        exchange_wait(s.send, c, s.sem_d.at[0, c])
 
 
 class Scratch:
@@ -476,21 +545,21 @@
     dma = pltpu.SemaphoreType.DMA
     scratch = dict(
         x=low(T, D), cot=low(T, D), wsq=low(D, 3 * D), wso=low(D, D), wtq=low(D, 3 * D), wto=low(D, D),
-        nrm=low(T, D), qkv=low(T, 3 * D), att=low(T, D), low=low(T, D), low_t=low(D, T),
+        qkv=low(T, 3 * D), att=low(T, D), low=low(T, D), low_t=low(D, T),
         tqkv=low(T, 3 * D), da=low(T, D), dqkv=low(T, 3 * D), bias=pltpu.VMEM((CLIP, CLIP), F32),
-        send_s=low(2, 32, 8, D), recv_s=low(2, 32, 8, D),
-        send_d=low(2, 32, 8, D), recv_d=low(2, 32, 8, D),
+        send=low(2, 32, 8, D), recv_s=low(2, 32, 8, D),
+        recv_d=low(2, 32, 8, D),
         give=low(4, 2, 256, 768), take=low(4, 2, 256, 768), held=low(4, 2, 256, 768),
         rb=low(4, 3, 2, 64, 768), ra=low(4, 3, 2, 16, 768), rz=low(4, 4, 16, 768),
-        total=low(4, 256, 768),
-        local=dma((6,)), send=dma((COPIES,)), recv=dma((COPIES,)), sem_s=dma((2, 2)), sem_d=dma((2, 2)),
+        total=low(4, 256, 768), rx=low(2, 256, 768), grad=pltpu.VMEM((T, D), F32),
+        local=dma((6,)), sent=dma((COPIES,)), got=dma((COPIES,)), sem_s=dma((2, 2)), sem_d=dma((2, 2)),
     )
     names = ["x_hbm", "sp_qkv", "sp_out", "tm_qkv", "tm_out", "cot_hbm", "block_out", "gin", "gtm"]
     block_out, grad_in, grad_tm = pl.pallas_call(
         functools.partial(kernel, names + list(scratch)),
         out_shape=[
             jax.ShapeDtypeStruct((T, D), BF16),
-            jax.ShapeDtypeStruct((T, D), F32),
+            jax.ShapeDtypeStruct((T, D), BF16),
             jax.ShapeDtypeStruct((256, 3 * D), F32),
         ],
         in_specs=[ANY] * 6,
@@ -501,10 +570,10 @@
         ),
         name="block",
     )(frames_in.reshape(T, D), sp_qkv, sp_out, tm_qkv, tm_out, cotangent.reshape(T, D))
-    return (block_out.reshape(cotangent.shape), grad_in.reshape(frames_in.shape), grad_tm)
-
-
-COPIES = 6 * 12 + 4 * 16
+    return (block_out.reshape(cotangent.shape), grad_in.reshape(frames_in.shape).astype(F32), grad_tm)
+
+
+COPIES = 200
 
 
 def solution(mesh):

time: 170 us -> 140 us (0.82)
  Pallas kernels: 163 us -> 134 us
  local copies, waits for them, and re-layouts: 6.72 us -> 2.64 us
  other arithmetic: 0 us -> 2.94 us
    pallas_call x1, Pallas kernels: 163 us -> 134 us  [body(): pl.pallas_call(functools.partial(kernel, names + list(scratch)), out_shap...]
    unnamed x7 -> x6, local copies, waits for them, and re-layouts: 6.72 us -> 2.64 us
    unnamed x0 -> x1, other arithmetic: none -> 2.94 us
where the time goes in v4:
time: 140 us
  Pallas kernels  134 us (96%)
  other arithmetic  2.94 us (2%)
  local copies, waits for them, and re-layouts  2.64 us (2%)
    pallas_call x1, Pallas kernels, body(): pl.pallas_call(functools.partial(kernel, names + list(scratch)), out_shap...  134 us
    unnamed x1, other arithmetic  2.94 us

profile of v4, /device:TPU:0, one launch (start us, length us, event | category | flops | bytes accessed | tf_op | source)
XLA Modules:
  0.0 140.0 jit_solution(7222685879575512192)
XLA Ops:
  0.6 133.8 %block.1 = (bf16[512,1024]{1,0:T(8,128)(2,1)}, bf16[512,1024]{1,0:T(8,128)(2,1)}, f32[256,3072]{1,0:T(8,128)}) custom-call(bf16[512,1024]{1,0:T(8,128)(2,1)} %bitcast.10, bf16[256,3072]{1,0:T(8,128)(2,1)} %refs_1_.1, bf16[256,1024]{1,0:T(8,128)(2,1)} %refs_2_.1, bf16[256,3072]{1,0:T(8,128)(2,1)} %refs_3_.1, bf16[256,1024]{1,0:T(8,128)(2,1)} %refs_4_.1, ...), custom_call_target="tpu_custom_call" | custom-call | tf_op jit(solution)/shard_map/block/pallas_call | solution.py:558
  134.4 0.0 copy-start.1
  134.4 0.0 copy-start
  134.4 2.9 %convert.2 = f32[2,1,256,1024]{3,2,1,0:T(8,128)} convert(bf16[2,1,256,1024]{3,2,1,0:T(8,128)(2,1)} %bitcast.8) | non-fusion elementwise | flops 524288 | bytes 3145728
  137.4 0.0 copy-done.1
  137.4 1.0 copy.12
  138.4 0.0 copy-done
  138.4 1.7 %copy.13 = f32[256,3072]{1,0:T(8,128)} copy(f32[256,3072]{1,0:T(8,128)S(1)} %copy-done) | data formatting | bytes 6291456
Async XLA Ops:
  134.4 3.0 %copy-start.1 = (bf16[512,1024]{1,0:T(8,128)(2,1)S(1)}, bf16[512,1024]{1,0:T(8,128)(2,1)}, u32[]{:S(2)}) copy-start(bf16[512,1024]{1,0:T(8,128)(2,1)} %get-tuple-element.6) | copy-start | bytes 3145732
  134.4 3.9 %copy-start = (f32[256,3072]{1,0:T(8,128)S(1)}, f32[256,3072]{1,0:T(8,128)}, u32[]{:S(2)}) copy-start(f32[256,3072]{1,0:T(8,128)} %get-tuple-element.17) | copy-start | bytes 9437188

commit v5 on v4

--- a/solution.py
+++ b/solution.py
@@ -122,10 +122,6 @@
         self.a_next, self.a_prev = self.at(self.ap, self.b), self.at(self.am, self.b)
         self.b_next, self.b_prev = self.at(self.a, self.bp), self.at(self.a, self.bm)
 
-    def across(self, a):
-        frame, _ = self.at(a, self.b)
-        return (frame + (1 - 2 * self.lo) * 16, (1 - self.hi) * 2 + self.core)
-
     def at(self, a, b):
         x = a + self.core * (b - a)
         y = b + self.core * (a - b)
@@ -170,24 +166,20 @@
     pltpu.make_async_copy(block, block, sem).wait()
 
 
-def gather(copies, here, shard, out, wide):
+def gather(copies, here, shard, out):
     own = here.fsdp * 256
     base = ((1 - here.hi) * 2 + here.core) * 256
     piece = (here.b * 4 + here.a) * 16
     row = (here.ap, here.am, here.a2)
     src, dst = shard.at[rows_at(piece, 16), :], out.at[rows_at(own + piece, 16), :]
-    sent = [copies.start(src, dst, here.cross)]
-    if wide:
-        sent += [copies.start(src, dst, here.across(a)) for a in row]
+    cross = copies.start(src, dst, here.cross)
+    yield
+    cross.wait_recv()
+    block = out.at[rows_at(base + piece, 16), :]
+    sent = [copies.start(block, block, here.at(a, here.b)) for a in row]
     yield
     for copy in sent:
         copy.wait_recv()
-    if not wide:
-        block = out.at[rows_at(base + piece, 16), :]
-        sent = [copies.start(block, block, here.at(a, here.b)) for a in row]
-        yield
-        for copy in sent:
-            copy.wait_recv()
     block = out.at[rows_at(base + here.b * 64, 64), :]
     sent = [copies.start(block, block, here.at(here.a, b)) for b in (here.bp, here.bm, here.b2)]
     over = [copies.start(block, block, here.sibling)]
@@ -200,6 +192,17 @@
     yield
     for copy in over:
         copy.wait_recv()
+
+
+def gather_whole(copies, here, shard, out):
+    own = rows_at(here.fsdp * 256, 256)
+    cross = copies.start(shard, out.at[own, :], here.cross)
+    yield
+    cross.wait_recv()
+    block = out.at[rows_at(((1 - here.hi) * 2 + here.core) * 256, 256), :]
+    over = copies.start(block, block, here.sibling)
+    yield
+    over.wait_recv()
 
 
 def gather_across(copies, here, shard, out):
@@ -238,7 +241,7 @@
         held[h] = (held[h].astype(F32) + take[h].astype(F32)).astype(BF16)
     shards, count = slice(None), 2
     if across_first:
-        rx = s.rx.at[g]
+        rx = s.rx.at[sum(ACROSS_FIRST[:g])]
         cross = copies.start(held.at[1 - here.hi], rx, here.cross)
         yield
         cross.wait_recv()
@@ -299,7 +302,9 @@
     for copy in sent:
         copy.wait_recv()
     for i in range(3):
-        s.gtm[:, pl.ds(i * D + g * 256, 256)] = total[:, pl.ds(i * 256, 256)].astype(F32)
+        cols = pl.ds(i * D + g * 256, 256)
+        s.gtm[:, cols] = total[:, pl.ds(i * 256, 256)].astype(F32)
+        pltpu.make_async_copy(s.gtm.at[:, cols], s.gtm_out.at[:, cols], s.local.at[6 + g * 3 + i]).start()
 
 
 def kernel(names, *refs):
@@ -324,8 +329,7 @@
         peer = lax.rem(here.frame + 1 + d, 32)
         pl.semaphore_signal(barrier, inc=1, device_id=(peer, here.fsdp), device_id_type=MESH)
 
-    near = [here.sibling, here.cross, here.far]
-    for device in near + [here.across(a) for a in (here.ap, here.am, here.a2)]:
+    for device in (here.sibling, here.cross, here.far):
         pl.semaphore_signal(barrier, inc=1, device_id=device, device_id_type=MESH)
     copies = Copies(s.sent, s.got)
 
@@ -341,13 +345,15 @@
     thirds = [pl.ds(i * D, D) for i in range(3)]
     halves = [[pl.ds(i * D + n * 512, 512) for i in range(3)] for n in range(2)]
     sp = [
-        [gather(copies, here, s.sp_qkv.at[:, c], s.wsq.at[:, c], n == 0) for c in halves[n]]
+        [gather(copies, here, s.sp_qkv.at[:, c], s.wsq.at[:, c]) for c in halves[n]]
         for n in range(2)
     ]
     sp_out = gather_across(copies, here, s.sp_out, s.wso)
-    tm = [gather_across(copies, here, s.tm_qkv.at[:, c], s.wtq.at[:, c]) for c in thirds[:2]]
-    tm.append(gather(copies, here, s.tm_qkv.at[:, thirds[2]], s.wtq.at[:, thirds[2]], False))
-    tm_out = gather_across(copies, here, s.tm_out, s.wto)
+    tm = [
+        how(copies, here, s.tm_qkv.at[:, c], s.wtq.at[:, c])
+        for how, c in zip((gather, gather_across, gather), thirds)
+    ]
+    tm_out = gather_whole(copies, here, s.tm_out, s.wto)
 
     loads[0].wait()
 
@@ -356,14 +362,14 @@
         rows = ds(r, 64)
         s.low[rows, :] = normalize(s.x[rows, :].astype(F32))[0].astype(BF16)
 
-    pl.semaphore_wait(barrier, 37)
+    pl.semaphore_wait(barrier, 34)
     step(*sp[0], *sp[1])
 
     def over(shard, out):
         return copies.start(shard, out.at[rows_at(here.fsdp * 256, 256), :], here.sibling)
 
     mine = [over(s.sp_qkv, s.wsq), over(s.sp_out, s.wso)]
-    step(sp_out, tm[2])
+    step(sp_out, *tm)
 
     row = lax.broadcasted_iota(jnp.int32, (CLIP, CLIP), 0)
     col = lax.broadcasted_iota(jnp.int32, (CLIP, CLIP), 1)
@@ -371,9 +377,10 @@
     s.bias[...] = jnp.where(allowed, 0.0, -1e30)
 
     step(*sp[0], *sp[1])
+    step(*sp[0])
     step(*sp[1])
-    step(sp_out)
-    step(tm[0], tm[1])
+    step(sp_out, tm_out)
+    step(tm[0], tm[2])
     step(*sp[0])
     mine[0].wait_recv()
     loads[1].wait()
@@ -384,25 +391,24 @@
             cols = halves[n][i]
             s.qkv[:, cols] = dot(s.low[...], s.wsq[:, cols]).astype(BF16)
 
-    def attend(n):
-        @loop(2)
-        def _(c):
-            rows = rows_at(c * CLIP, CLIP)
-            attention([(rows, n * 4 + j) for j in range(4)], s.qkv, att=s.att)
+    def attend(n, c):
+        rows = pl.ds(c * CLIP, CLIP)
+        attention([(rows, n * 4 + j) for j in range(4)], s.qkv, att=s.att)
 
     project(0)
     step(*sp[1])
-    step(tm[2])
-    attend(0)
+    step(tm[0], tm[2], tm[1])
+    attend(0, 0)
+    attend(0, 1)
     project(1)
     step(sp_out)
-    step(tm[2], tm[0], tm[1], tm_out)
     mine += [over(s.tm_qkv, s.wtq), over(s.tm_out, s.wto)]
-    attend(1)
-    drain(sp_out)
-    mine[1].wait_recv()
-    loads[2].wait()
     for c in range(2):
+        attend(1, c)
+        if c == 0:
+            drain(sp_out)
+            mine[1].wait_recv()
+            loads[2].wait()
         rows = pl.ds(c * CLIP, CLIP)
 
         @loop(4)
@@ -413,7 +419,8 @@
 
         exchange_start(here, s.send, s.recv_s, c, s.sem_s)
 
-    step(tm_out, tm[0], tm[1], tm[2], tm_out)
+    step(tm_out)
+    step(*tm)
     drain(*tm, tm_out)
     mine[2].wait_recv()
     mine[3].wait_recv()
@@ -436,24 +443,28 @@
 
         rows = pl.ds(c * CLIP, CLIP)
         s.low_t[:, rows] = s.low[rows, :].T
-
-    def pump(*which):
-        for g in which:
+        if c == 0:
+
+            @loop(6)
+            def _(n):
+                cols = ds(n, 512)
+                s.tqkv[:CLIP, cols] = dot(s.low[:CLIP, :], s.wtq[:, cols]).astype(BF16)
+
+    def pump(point):
+        for g in PLAN.get(point, ()):
             next(chunks[g], None)
 
-    chunks = [reduce_chunk(copies, here, s, g, g < 2) for g in range(4)]
+    chunks = [reduce_chunk(copies, here, s, g, ACROSS_FIRST[g]) for g in range(4)]
     for g in range(4):
 
-        @loop(3)
-        def _(i):
-            cols = pl.ds(pl.multiple_of(i * D + g * 256, 256), 256)
-            s.tqkv[:, cols] = dot(s.low[...], s.wtq[:, cols]).astype(BF16)
+        for i in range(3):
+            cols = pl.ds(i * D + g * 256, 256)
+            s.tqkv[CLIP:, cols] = dot(s.low[CLIP:, :], s.wtq[:, cols]).astype(BF16)
 
         units = [(pl.ds(c * CLIP, CLIP), g * 2 + n) for n in range(2) for c in range(2)]
         attention(units, s.tqkv, s.bias, s.att, s.da, s.dqkv)
         step(chunks[g])
-        if g > 0:
-            step(chunks[g - 1])
+        pump(f"group{g}")
 
     for c in range(2):
         rows = pl.ds(c * CLIP, CLIP)
@@ -463,7 +474,7 @@
             cols = ds(n, 256)
             s.grad[rows, cols] = dot_nt(s.dqkv[rows, :], s.wtq[cols, :])
 
-        pump(*((3, 0), (2,))[c])
+        pump(f"grad{c}")
         exchange_wait(s.send, c, s.sem_s.at[0, c])
 
         @loop(4)
@@ -484,7 +495,12 @@
             stream = s.recv_s[c, :, :, cols].astype(F32).reshape(CLIP, 512)
             s.block_out[rows, cols] = (dot(s.att[rows, :], s.wto[:, cols]) + stream).astype(BF16)
 
-        pump(*((0,), (2, 1))[c])
+        rows = pl.ds(c * CLIP, CLIP)
+        pltpu.make_async_copy(
+            s.block_out.at[rows, :], s.block_out_out.at[rows, :], s.local.at[20 + c]
+        ).start()
+
+        pump(f"out{c}")
 
     for c in range(2):
         rows = pl.ds(c * CLIP, CLIP)
@@ -500,33 +516,46 @@
             cols = ds(n, 512)
             s.da[rows, cols] = dot_nt(s.low[rows, :], s.wso[cols, :]).astype(BF16)
 
-        pump(*((3, 0), ())[c])
+        pump(f"att{c}")
 
         for g in range(2):
 
             units = [(rows, g * 4 + n) for n in range(4)]
             attention(units, s.qkv, d_att=s.da, d_qkv=s.tqkv)
-            pump(*((2,), (1, 3, 0), (1, 3, 2), (0,))[c * 2 + g])
+            pump(f"heads{c}{g}")
 
         @loop(4)
         def _(n):
             cols = ds(n, 256)
             s.grad[rows, cols] = dot_nt(s.tqkv[rows, :], s.wsq[cols, :])
 
-        pump(*((2,), (1, 3))[c])
+        pump(f"in{c}")
 
         @loop(4)
         def _(r):
             rows = rows_at(c * CLIP + r * 64, 64)
             normed, rstd = normalize(s.x[rows, :].astype(F32))
             grad = s.low[rows, :].astype(F32) + norm_back(normed, rstd, s.grad[rows, :])
-            s.gin[rows, :] = grad.astype(BF16)
-
-        pump(*((3, 1, 0), (1,))[c])
+            s.grad[rows, :] = grad
+
+        pltpu.make_async_copy(s.grad.at[rows, :], s.gin_out.at[rows, :], s.local.at[18 + c]).start()
+
+        pump(f"norm{c}")
 
     drain(*chunks)
     copies.finish()
+    for g in range(4):
+        for i in range(3):
+            cols = pl.ds(i * D + g * 256, 256)
+            pltpu.make_async_copy(
+                s.gtm.at[:, cols], s.gtm_out.at[:, cols], s.local.at[6 + g * 3 + i]
+            ).wait()
     for c in range(2):
+        rows = pl.ds(c * CLIP, CLIP)
+        pltpu.make_async_copy(s.grad.at[rows, :], s.gin_out.at[rows, :], s.local.at[18 + c]).wait()
+        pltpu.make_async_copy(
+            s.block_out.at[rows, :], s.block_out_out.at[rows, :], s.local.at[20 + c]
+        ).wait()
         exchange_wait(s.send, c, s.sem_d.at[0, c])
 
 
@@ -536,7 +565,6 @@
             setattr(self, name, ref)
 
 
-VM = pl.BlockSpec(memory_space=pltpu.VMEM)
 ANY = pl.BlockSpec(memory_space=pl.ANY)
 
 
@@ -552,28 +580,34 @@
         give=low(4, 2, 256, 768), take=low(4, 2, 256, 768), held=low(4, 2, 256, 768),
         rb=low(4, 3, 2, 64, 768), ra=low(4, 3, 2, 16, 768), rz=low(4, 4, 16, 768),
         total=low(4, 256, 768), rx=low(2, 256, 768), grad=pltpu.VMEM((T, D), F32),
-        local=dma((6,)), sent=dma((COPIES,)), got=dma((COPIES,)), sem_s=dma((2, 2)), sem_d=dma((2, 2)),
+        local=dma((22,)), block_out=low(T, D), gtm=pltpu.VMEM((256, 3 * D), F32), sent=dma((COPIES,)), got=dma((COPIES,)), sem_s=dma((2, 2)), sem_d=dma((2, 2)),
     )
-    names = ["x_hbm", "sp_qkv", "sp_out", "tm_qkv", "tm_out", "cot_hbm", "block_out", "gin", "gtm"]
+    names = ["x_hbm", "sp_qkv", "sp_out", "tm_qkv", "tm_out", "cot_hbm", "block_out_out", "gin_out", "gtm_out"]
     block_out, grad_in, grad_tm = pl.pallas_call(
         functools.partial(kernel, names + list(scratch)),
         out_shape=[
             jax.ShapeDtypeStruct((T, D), BF16),
-            jax.ShapeDtypeStruct((T, D), BF16),
+            jax.ShapeDtypeStruct((T, D), F32),
             jax.ShapeDtypeStruct((256, 3 * D), F32),
         ],
         in_specs=[ANY] * 6,
-        out_specs=[VM] * 3,
+        out_specs=[ANY] * 3,
         scratch_shapes=list(scratch.values()),
         compiler_params=pltpu.CompilerParams(
             vmem_limit_bytes=VMEM_LIMIT, collective_id=0, has_side_effects=True
         ),
         name="block",
     )(frames_in.reshape(T, D), sp_qkv, sp_out, tm_qkv, tm_out, cotangent.reshape(T, D))
-    return (block_out.reshape(cotangent.shape), grad_in.reshape(frames_in.shape).astype(F32), grad_tm)
+    return (block_out.reshape(cotangent.shape), grad_in.reshape(frames_in.shape), grad_tm)
 
 
 COPIES = 200
+ACROSS_FIRST = (False, False, True, True)
+PLAN = dict(
+    group1=(0,), group2=(1,), group3=(2,), grad0=(3,), grad1=(0,), out0=(1,), out1=(0,),
+    att0=(2, 1), heads00=(0,), heads01=(1, 3), in0=(2, 0), norm0=(3, 1), att1=(2, 0),
+    heads10=(3, 1), heads11=(2,), in1=(3, 2), norm1=(3, 2),
+)
 
 
 def solution(mesh):

time: 140 us -> 127 us (0.907)
  Pallas kernels: 134 us -> 120 us
  local copies, waits for them, and re-layouts: 2.64 us -> 6.72 us
  other arithmetic: 2.94 us -> 0 us
    pallas_call x1, Pallas kernels: 134 us -> 120 us  [body(): pl.pallas_call(functools.partial(kernel, names + list(scratch)), out_shap...]
    unnamed x6 -> x7, local copies, waits for them, and re-layouts: 2.64 us -> 6.72 us
    unnamed x1 -> x0, other arithmetic: 2.94 us -> none
where the time goes in v5:
time: 127 us
  Pallas kernels  120 us (94%)
  local copies, waits for them, and re-layouts  6.72 us (5%)
    pallas_call x1, Pallas kernels, body(): pl.pallas_call(functools.partial(kernel, names + list(scratch)), out_shap...  120 us
    unnamed x7, local copies, waits for them, and re-layouts  6.72 us

profile of v5, /device:TPU:0, one launch (start us, length us, event | category | flops | bytes accessed | tf_op | source)
XLA Modules:
  0.0 127.3 jit_solution(16439167629988379744)
XLA Ops:
  0.6 119.9 %block.1 = (bf16[512,1024]{1,0:T(8,128)(2,1)}, f32[512,1024]{1,0:T(8,128)}, f32[256,3072]{1,0:T(8,128)}) custom-call(bf16[512,1024]{1,0:T(8,128)(2,1)} %bitcast.8, bf16[256,3072]{1,0:T(8,128)(2,1)} %refs_1_.1, bf16[256,1024]{1,0:T(8,128)(2,1)} %refs_2_.1, bf16[256,3072]{1,0:T(8,128)(2,1)} %refs_3_.1, bf16[256,1024]{1,0:T(8,128)(2,1)} %refs_4_.1, ...), custom_call_target="tpu_custom_call" | custom-call | tf_op jit(solution)/shard_map/block/pallas_call | solution.py:586
  120.6 0.0 copy-start.1
  120.6 2.4 %copy.13 = bf16[2,32,8,1024]{3,2,1,0:T(8,128)(2,1)} copy(bf16[2,32,8,1024]{3,2,1,0:T(8,128)(2,1)} %bitcast.7) | data formatting | bytes 2097152
  123.0 0.0 copy-done.1
  123.0 0.0 copy-start
  123.0 1.3 %copy.14 = f32[2,1,256,1024]{3,2,1,0:T(8,128)} copy(f32[2,1,256,1024]{3,2,1,0:T(8,128)S(1)} %bitcast.6) | data formatting | bytes 4194304
  124.3 1.3 %copy-done = f32[256,3072]{1,0:T(8,128)S(1)} copy-done((f32[256,3072]{1,0:T(8,128)S(1)}, f32[256,3072]{1,0:T(8,128)}, u32[]{:S(2)}) %copy-start) | copy-done | bytes 3145752
  125.6 1.7 %copy.15 = f32[256,3072]{1,0:T(8,128)} copy(f32[256,3072]{1,0:T(8,128)S(1)} %copy-done) | data formatting | bytes 6291456
Async XLA Ops:
  120.6 2.4 %copy-start.1 = (f32[512,1024]{1,0:T(8,128)S(1)}, f32[512,1024]{1,0:T(8,128)}, u32[]{:S(2)}) copy-start(f32[512,1024]{1,0:T(8,128)} %get-tuple-element.7) | copy-start | bytes 6291460
  123.0 2.6 %copy-start = (f32[256,3072]{1,0:T(8,128)S(1)}, f32[256,3072]{1,0:T(8,128)}, u32[]{:S(2)}) copy-start(f32[256,3072]{1,0:T(8,128)} %get-tuple-element.17) | copy-start | bytes 9437188

commit v6 on v5

--- a/solution.py
+++ b/solution.py
@@ -542,7 +542,9 @@
 
         pump(f"norm{c}")
 
-    drain(*chunks)
+    for _ in range(8):
+        for steps in chunks:
+            next(steps, None)
     copies.finish()
     for g in range(4):
         for i in range(3):
@@ -604,9 +606,9 @@
 COPIES = 200
 ACROSS_FIRST = (False, False, True, True)
 PLAN = dict(
-    group1=(0,), group2=(1,), group3=(2,), grad0=(3,), grad1=(0,), out0=(1,), out1=(0,),
-    att0=(2, 1), heads00=(0,), heads01=(1, 3), in0=(2, 0), norm0=(3, 1), att1=(2, 0),
-    heads10=(3, 1), heads11=(2,), in1=(3, 2), norm1=(3, 2),
+    group1=(0,), group2=(1,), group3=(2,), grad0=(3,), out1=(0, 1), heads00=(0, 1, 2),
+    heads01=(0, 1, 3), in0=(2, 0, 1), att1=(3, 2, 0, 1), heads10=(3, 2), heads11=(3, 2),
+    in1=(3, 2), norm1=(3, 2),
 )
 
 

time: 127 us -> 126 us (level)
  Pallas kernels: 120 us -> 118 us
    pallas_call x1, Pallas kernels: 120 us -> 118 us  [body(): pl.pallas_call(functools.partial(kernel, names + list(scratch)), out_shap...]
where the time goes in v6:
time: 126 us
  Pallas kernels  118 us (94%)
  local copies, waits for them, and re-layouts  6.72 us (5%)
    pallas_call x1, Pallas kernels, body(): pl.pallas_call(functools.partial(kernel, names + list(scratch)), out_shap...  118 us
    unnamed x7, local copies, waits for them, and re-layouts  6.72 us

profile of v6, /device:TPU:0, one launch (start us, length us, event | category | flops | bytes accessed | tf_op | source)
XLA Modules:
  0.0 125.6 jit_solution(11828093950039392951)
XLA Ops:
  0.6 118.2 %block.1 = (bf16[512,1024]{1,0:T(8,128)(2,1)}, f32[512,1024]{1,0:T(8,128)}, f32[256,3072]{1,0:T(8,128)}) custom-call(bf16[512,1024]{1,0:T(8,128)(2,1)} %bitcast.8, bf16[256,3072]{1,0:T(8,128)(2,1)} %refs_1_.1, bf16[256,1024]{1,0:T(8,128)(2,1)} %refs_2_.1, bf16[256,3072]{1,0:T(8,128)(2,1)} %refs_3_.1, bf16[256,1024]{1,0:T(8,128)(2,1)} %refs_4_.1, ...), custom_call_target="tpu_custom_call" | custom-call | tf_op jit(solution)/shard_map/block/pallas_call | solution.py:588
  118.9 0.0 copy-start.1
  118.9 2.4 %copy.13 = bf16[2,32,8,1024]{3,2,1,0:T(8,128)(2,1)} copy(bf16[2,32,8,1024]{3,2,1,0:T(8,128)(2,1)} %bitcast.7) | data formatting | bytes 2097152
  121.3 0.0 copy-done.1
  121.3 0.0 copy-start
  121.3 1.3 %copy.14 = f32[2,1,256,1024]{3,2,1,0:T(8,128)} copy(f32[2,1,256,1024]{3,2,1,0:T(8,128)S(1)} %bitcast.6) | data formatting | bytes 4194304
  122.6 1.3 %copy-done = f32[256,3072]{1,0:T(8,128)S(1)} copy-done((f32[256,3072]{1,0:T(8,128)S(1)}, f32[256,3072]{1,0:T(8,128)}, u32[]{:S(2)}) %copy-start) | copy-done | bytes 3145752
  123.9 1.7 %copy.15 = f32[256,3072]{1,0:T(8,128)} copy(f32[256,3072]{1,0:T(8,128)S(1)} %copy-done) | data formatting | bytes 6291456
Async XLA Ops:
  118.9 2.4 %copy-start.1 = (f32[512,1024]{1,0:T(8,128)S(1)}, f32[512,1024]{1,0:T(8,128)}, u32[]{:S(2)}) copy-start(f32[512,1024]{1,0:T(8,128)} %get-tuple-element.7) | copy-start | bytes 6291460
  121.3 2.6 %copy-start = (f32[256,3072]{1,0:T(8,128)S(1)}, f32[256,3072]{1,0:T(8,128)}, u32[]{:S(2)}) copy-start(f32[256,3072]{1,0:T(8,128)} %get-tuple-element.17) | copy-start | bytes 9437188
